TPU v7x, 32 devices: a whole 2x2x4 slice. The times are simulated.
32 devices in a mesh: ctx: 8 (over z, x), head: 4 (over y, core).
Axes of the slice: x: 2, y: 2, z: 4, core: 2. Of those that a mesh axis runs over, the one named last changes fastest.
Arguments:
- latent: bfloat16 [2048, 576], P('ctx'), may hold values from -8 to 8
- query: bfloat16 [2048, 12288], P('ctx', 'head'), may hold values from -300 to 300
- d_out: bfloat16 [2048, 8192], P('ctx', 'head'), may hold values from -6 to 6
- w_uk: bfloat16 [64, 128, 512], P('head'), may hold values from -0.5 to 0.5
- w_uv: bfloat16 [64, 128, 512], P('head'), may hold values from -0.25 to 0.25
- block_mask: int32 [8, 8], replicated, may hold values 0 or 1
- segments: int32 [2048], replicated, may hold values from 0 to 3, never falling along the last dimension, each value on 1 to 1536 neighbouring positions
Outputs:
- attended: bfloat16 [2048, 8192], P('ctx', 'head')
- d_query: bfloat16 [2048, 12288], P('ctx', 'head')
- d_latent: float32 [2048, 576], P('ctx')
- d_w_uk: float32 [64, 128, 512], P('head')
- d_w_uv: float32 [64, 128, 512], P('head')
Inputs may be any that keep to these rules, and one draw needn't show every extreme that they name: block_mask[a, b] = 1 lets every token of block a read every earlier token of block b whatever their dialogues. `segments`: dialogue ids never fall along the sequence; each dialogue holds 1 to 1536 tokens and one holds exactly 1536.
All inputs are finite; a program needn't handle non-finite values.
Results may differ from a plain program's by a relative error of at most 0.012.
The roundings to bfloat16 on the way count: a program that leaves them out, or rounds other values in their place, can miss the bound.
Values may be sent and summed in bfloat16 or wider, within the bound.
A program may use at most 256 MiB of HBM per device.

v0:
```python
import math

import jax
import jax.numpy as jnp
from jax import lax
from jax.sharding import PartitionSpec as P

SPAN = 2


def shifted(block, axis, distance):
    devices = range(lax.axis_size(axis))
    route = [(i - distance, i) for i in devices if i - distance in devices]
    return lax.ppermute(block, axis, route)


def body(latent, query, d_out, w_uk, w_uv, block_mask, segments):
    tok_rows = latent.shape[0]
    lat_width = latent.shape[1]
    heads_here = w_uk.shape[0]
    nope_width = w_uk.shape[1]
    rank_width = w_uk.shape[2]
    value_width = w_uv.shape[1]
    query_width = query.shape[1] // heads_here
    rope_width = query_width - nope_width
    inv_root = 1.0 / math.sqrt(query_width)
    position = lax.axis_index("ctx")
    queries = query.reshape(tok_rows, heads_here, query_width)
    q_nope = queries[:, :, :nope_width]
    q_rope = queries[:, :, nope_width:]
    absorbed = jnp.einsum("thn,hnr->thr", q_nope, w_uk, preferred_element_type=jnp.float32).astype(
        jnp.bfloat16
    )
    q_full = jnp.concatenate([absorbed, q_rope], axis=2)
    key_blocks = [latent]
    current = latent
    for cycle_step in range(SPAN):
        current = shifted(current, "ctx", 1)
        key_blocks.append(current)
    offsets = jnp.arange(tok_rows, dtype=jnp.int32)
    seg_query = lax.dynamic_slice_in_dim(segments, position * tok_rows, tok_rows)
    q_pos = position * tok_rows + offsets
    masks = []
    actives = []
    for cycle_step in range(SPAN + 1):
        key_block = position - cycle_step
        clamped = jnp.maximum(key_block, 0)
        seg_key = lax.dynamic_slice_in_dim(segments, clamped * tok_rows, tok_rows)
        granted = block_mask[position, clamped]
        k_pos = key_block * tok_rows + offsets
        allowed = (
            (key_block >= 0)
            & (k_pos[None, :] <= q_pos[:, None])
            & ((seg_query[:, None] == seg_key[None, :]) | (granted == 1))
        )
        masks.append(allowed)
        if cycle_step == 0:
            actives.append(jnp.array(True))
        else:
            actives.append(
                (key_block >= 0) & ((granted == 1) | (seg_key[tok_rows - 1] == seg_query[0]))
            )
    score_list = []
    for cycle_step in range(SPAN + 1):

        def score_fn(block_keys=key_blocks[cycle_step]):
            return (
                jnp.einsum("thl,kl->htk", q_full, block_keys, preferred_element_type=jnp.float32)
                * inv_root
            )

        raw_scores = score_fn()
        score_list.append(jnp.where(masks[cycle_step][None], raw_scores, -jnp.inf))
    scores = jnp.concatenate(score_list, axis=2)
    row_max = jnp.max(scores, axis=2, keepdims=True)
    weights = jnp.exp(scores - row_max)
    probs = weights / jnp.sum(weights, axis=2, keepdims=True)
    probs_low = probs.astype(jnp.bfloat16)
    prob_blocks = [
        probs_low[:, :, cycle_step * tok_rows : (cycle_step + 1) * tok_rows]
        for cycle_step in range(SPAN + 1)
    ]
    out_shape = (tok_rows, heads_here, rank_width)
    latent_sum = jnp.zeros(out_shape, jnp.float32)
    for cycle_step in range(SPAN + 1):

        def value_fn(block_probs=prob_blocks[cycle_step], block_keys=key_blocks[cycle_step]):
            return jnp.einsum(
                "htk,kr->thr",
                block_probs,
                block_keys[:, :rank_width],
                preferred_element_type=jnp.float32,
            )

        latent_sum = latent_sum + value_fn()
    latent_out = latent_sum.astype(jnp.bfloat16)
    attended = jnp.einsum(
        "thr,hvr->thv", latent_out, w_uv, preferred_element_type=jnp.float32
    ).astype(jnp.bfloat16)
    grads = d_out.reshape(tok_rows, heads_here, value_width)
    d_latent_out = jnp.einsum(
        "thv,hvr->thr", grads, w_uv, preferred_element_type=jnp.float32
    ).astype(jnp.bfloat16)
    grad_uv = jnp.einsum("thv,thr->hvr", grads, latent_out, preferred_element_type=jnp.float32)
    dprob_list = []
    for cycle_step in range(SPAN + 1):

        def dprob_fn(block_keys=key_blocks[cycle_step]):
            return jnp.einsum(
                "thr,kr->htk",
                d_latent_out,
                block_keys[:, :rank_width],
                preferred_element_type=jnp.float32,
            )

        dprob_list.append(dprob_fn())
    d_probs = jnp.concatenate(dprob_list, axis=2)
    delta = jnp.sum(probs * d_probs, axis=2, keepdims=True)
    d_scores = (probs * (d_probs - delta) * inv_root).astype(jnp.bfloat16)
    dscore_blocks = [
        d_scores[:, :, cycle_step * tok_rows : (cycle_step + 1) * tok_rows]
        for cycle_step in range(SPAN + 1)
    ]
    full_shape = (tok_rows, heads_here, lat_width)
    d_full = jnp.zeros(full_shape, jnp.float32)
    key_parts = []
    for cycle_step in range(SPAN + 1):

        def dquery_fn(block_grads=dscore_blocks[cycle_step], block_keys=key_blocks[cycle_step]):
            return jnp.einsum(
                "htk,kl->thl", block_grads, block_keys, preferred_element_type=jnp.float32
            )

        def dkey_fn(block_grads=dscore_blocks[cycle_step], block_probs=prob_blocks[cycle_step]):
            from_scores = jnp.einsum(
                "htk,thl->kl", block_grads, q_full, preferred_element_type=jnp.float32
            )
            from_values = jnp.einsum(
                "htk,thr->kr", block_probs, d_latent_out, preferred_element_type=jnp.float32
            )
            return from_scores + jnp.pad(from_values, ((0, 0), (0, rope_width)))

        d_full = d_full + dquery_fn()
        key_parts.append(dkey_fn())
    d_absorbed = d_full[:, :, :rank_width].astype(jnp.bfloat16)
    d_nope = jnp.einsum("thr,hnr->thn", d_absorbed, w_uk, preferred_element_type=jnp.float32)
    d_query = jnp.concatenate([d_nope, d_full[:, :, rank_width:]], axis=2).astype(jnp.bfloat16)
    grad_uk = jnp.einsum("thn,thr->hnr", q_nope, d_absorbed, preferred_element_type=jnp.float32)
    returned = jnp.zeros((tok_rows, lat_width), jnp.float32)
    for cycle_step in range(1, SPAN + 1):
        returned = returned + shifted(
            key_parts[cycle_step].astype(jnp.bfloat16), "ctx", -cycle_step
        ).astype(jnp.float32)
    d_latent = lax.psum(key_parts[0] + returned, "head")
    d_w_uk, d_w_uv = lax.psum((grad_uk, grad_uv), "ctx")
    return (
        attended.reshape(tok_rows, heads_here * value_width),
        d_query.reshape(tok_rows, heads_here * query_width),
        d_latent,
        d_w_uk,
        d_w_uv,
    )


def solution(mesh):
    in_specs = (
        P("ctx", None),
        P("ctx", "head"),
        P("ctx", "head"),
        P("head", None, None),
        P("head", None, None),
        P(),
        P(),
    )
    out_specs = (
        P("ctx", "head"),
        P("ctx", "head"),
        P("ctx", None),
        P("head", None, None),
        P("head", None, None),
    )
    return jax.shard_map(body, mesh=mesh, in_specs=in_specs, out_specs=out_specs, check_vma=False)
```

profile of v0, /device:TPU:14, one launch (start us, length us, event | category | flops | bytes accessed | tf_op | source)
XLA Modules:
  0.0 438.9 jit_solution(4890811326513276224)
XLA Ops:
  7.2 3.6 collective-permute-start
  14.2 2.6 copy.46
  18.8 4.5 %convert_bitcast_fusion = bf16[256,16,512]{0,2,1:T(8,128)(2,1)} fusion(bf16[16,128,512]{2,1,0:T(8,128)(2,1)S(1)} %copy-done, bf16[256,16,192]{0,2,1:T(8,128)(2,1)} %bitcast.144), kind=kOutput, calls=%fused_computation.29 | convolution fusion | flops 538968064 | bytes 7340032 | tf_op jit(solution)/shard_map/thn,hnr->thr/dot_general | solution.py:31
  23.3 3.0 convolution_convert_fusion
  29.0 3.4 fusion.25
  32.3 3.4 collective-permute-start.1
  35.7 3.0 fusion.126
  38.7 4.5 %fusion.28 = f32[16,256,256]{1,2,0:T(8,128)} fusion(bf16[16,512,256]{2,1,0:T(8,128)(2,1)S(1)} %convolution_convert_fusion, bf16[256,576]{0,1:T(8,128)(2,1)} %collective-permute-done), kind=kOutput, calls=%fused_computation.36 | convolution fusion | flops 1073741824 | bytes 8650752 | tf_op jit(solution)/shard_map/thr,kr->htk/dot_general | solution.py:109
  52.2 5.5 %fusion.51 = f32[16,256,512]{2,1,0:T(8,128)} fusion(bf16[16,256,768]{1,2,0:T(8,128)(2,1)S(1)} %fusion.121, bf16[256,576]{0,1:T(8,128)(2,1)} %collective-permute-done), kind=kOutput, calls=%fused_computation.54 | convolution fusion | flops 1073741824 | bytes 10747904 | tf_op jit(solution)/shard_map/htk,kr->thr/dot_general | solution.py:88
  57.7 5.6 %fusion.8 = bf16[256,16,512]{2,0,1:T(8,128)(2,1)S(1)} fusion(f32[16,256,512]{2,1,0:T(8,128)S(1)} %fusion.54, f32[16,256,512]{2,1,0:T(8,128)} %fusion.51, bf16[16,256,768]{1,2,0:T(8,128)(2,1)} %copy-done.4, bf16[256,576]{0,1:T(8,128)(2,1)S(1)} %collective-permute-done.1), kind=kOutput, calls=%fused_computation.13 | convolution fusion | flops 1080033280 | bytes 23330816 | tf_op jit(solution)/shard_map/htk,kr->thr/dot_general | solution.py:88
  63.3 3.4 convolution_bitcast_fusion
  66.8 3.4 fusion.31
  70.1 20.8 %multiply_convert_fusion = bf16[16,256,768]{1,2,0:T(8,128)(2,1)} fusion(f32[16,256,256]{1,2,0:T(8,128)} %fusion.31, f32[16,256,256]{1,2,0:T(8,128)} %fusion.28, f32[16,256,256]{1,2,0:T(8,128)} %fusion.25, f32[16,256]{1,0:T(8,128)S(1)} %fusion.6, f32[16,256]{1,0:T(8,128)S(1)} %maximum_maximum_fusion, f32[16,256,256]{1,2,0:T(8,128)} %copy-done.8, ...), kind=kOutput, calls=%fused_computation.4 | output fusion | flops 53482240 | bytes 31490048 | tf_op jit(solution)/shard_map/sub | solution.py:119
  91.0 3.1 fusion.46
  94.4 6.0 %fusion.42 = f32[16,256,576]{1,2,0:T(8,128)} fusion(bf16[16,256,768]{1,2,0:T(8,128)(2,1)S(1)} %copy-done.9, bf16[256,576]{0,1:T(8,128)(2,1)} %collective-permute-done), kind=kOutput, calls=%fused_computation.45 | convolution fusion | flops 1207959552 | bytes 11829248 | tf_op jit(solution)/shard_map/htk,kl->thl/dot_general | solution.py:130
  100.4 6.2 %fusion.7 = bf16[256,16,576]{0,2,1:T(8,128)(2,1)S(1)} fusion(f32[16,256,576]{1,2,0:T(8,128)S(1)} %fusion.46, f32[16,256,576]{1,2,0:T(8,128)} %fusion.42, bf16[16,256,768]{1,2,0:T(8,128)(2,1)} %multiply_convert_fusion, bf16[256,576]{0,1:T(8,128)(2,1)S(1)} %collective-permute-done.1), kind=kOutput, calls=%fused_computation.11 | convolution fusion | flops 1215037440 | bytes 25985024 | tf_op jit(solution)/shard_map/htk,kl->thl/dot_general | solution.py:130
  106.7 2.2 copy-done.5
  108.9 3.2 fusion.34
  112.2 4.3 fusion.76
  116.5 5.1 %fusion.95 = bf16[256,576]{0,1:T(8,128)(2,1)S(1)} fusion(bf16[16,256,768]{1,2,0:T(8,128)(2,1)} %multiply_convert_fusion, f32[256,512]{0,1:T(8,128)S(1)} %fusion.76, bf16[256,16,64]{0,2,1:T(8,128)(2,1)S(1)} %copy-done.18, bf16[256,16,512]{0,2,1:T(8,128)(2,1)} %convert_bitcast_fusion), kind=kOutput, calls=%fused_computation.72 | convolution fusion | flops 1217691648 | bytes 7634944 | tf_op jit(solution)/shard_map/htk,thl->kl/dot_general | solution.py:135
  121.7 3.5 collective-permute-start.2
  133.0 11.7 %collective-permute-done.2 = bf16[256,576]{0,1:T(8,128)(2,1)S(1)} collective-permute-done((bf16[256,576]{0,1:T(8,128)(2,1)S(1)}, bf16[256,576]{0,1:T(8,128)(2,1)S(1)}, u32[]{:S(2)}, u32[]{:S(2)}) %collective-permute-start.2) | collective-permute-done | bytes 294944 | tf_op jit(solution)/shard_map/ppermute | solution.py:14
  144.7 8.1 %collective-permute-done.3 = bf16[256,576]{0,1:T(8,128)(2,1)S(1)} collective-permute-done((bf16[256,576]{0,1:T(8,128)(2,1)S(1)}, bf16[256,576]{0,1:T(8,128)(2,1)S(1)}, u32[]{:S(2)}, u32[]{:S(2)}) %collective-permute-start.3) | collective-permute-done | bytes 294944 | tf_op jit(solution)/shard_map/ppermute | solution.py:14
  152.8 2.2 add_add_fusion
  155.1 5.4 %convolution_convert_fusion.1 = bf16[16,256,128]{1,2,0:T(8,128)(2,1)} fusion(bf16[256,16,512]{2,0,1:T(8,128)(2,1)} %copy-done.3, bf16[16,128,512]{2,1,0:T(8,128)(2,1)} %param.11), kind=kOutput, calls=%fused_computation.61 | convolution fusion | flops 537395200 | bytes 7340032 | tf_op jit(solution)/shard_map/thr,hvr->thv/dot_general | solution.py:97
  160.5 2.3 copy.77
  162.7 2.5 pad_maximum_fusion.3
  165.2 2.7 copy.78
  167.9 226.0 %all-reduce.9.cloned.1.call-done = (f32[16,128,512]{1,2,0:T(8,128)}, f32[16,128,512]{1,2,0:T(8,128)}) async-done(((f32[16,128,512]{1,2,0:T(8,128)}, f32[16,128,512]{1,2,0:T(8,128)}), (f32[16,128,512]{1,2,0:T(8,128)}, f32[16,128,512]{1,2,0:T(8,128)})) %all-reduce.9.cloned.1.call-update) | async-done | bytes 8388624 | tf_op jit(solution)/shard_map/psum | solution.py:155
  393.9 5.3 %copy.79 = f32[16,128,512]{2,1,0:T(8,128)} copy(f32[16,128,512]{1,2,0:T(8,128)} %get-tuple-element.15) | data formatting | bytes 8388608
  399.2 5.3 %copy.80 = f32[16,128,512]{2,1,0:T(8,128)} copy(f32[16,128,512]{1,2,0:T(8,128)} %get-tuple-element.16) | data formatting | bytes 8388608
  404.6 25.6 %all-reduce.7.cloned.1.call-done = f32[256,576]{0,1:T(8,128)} async-done(((f32[256,576]{0,1:T(8,128)}), f32[256,576]{0,1:T(8,128)}) %all-reduce.7.cloned.1.call-update) | async-done | bytes 589840 | tf_op jit(solution)/shard_map/psum | solution.py:154
  (79 shorter events, 24.8 us)
Async XLA Ops:
  7.2 11.6 %copy-start = (bf16[16,128,512]{2,1,0:T(8,128)(2,1)S(1)}, bf16[16,128,512]{2,1,0:T(8,128)(2,1)}, u32[]{:S(2)}) copy-start(bf16[16,128,512]{2,1,0:T(8,128)(2,1)} %param.10) | copy-start | bytes 6291460
  7.2 386.7 %all-reduce.9.cloned.1.call-start = ((), (), s32[]{:S(2)}) async-start(), calls=%async_computation.1 | async-start | bytes 16777216 | tf_op jit(solution)/shard_map/psum | solution.py:155
  7.2 25.1 %collective-permute-start = (bf16[256,576]{0,1:T(8,128)(2,1)}, bf16[256,576]{0,1:T(8,128)(2,1)}, u32[]{:S(2)}, u32[]{:S(2)}) collective-permute-start(bf16[256,576]{0,1:T(8,128)(2,1)} %param.7), channel_id=1, source_target_pairs={{0,4},{4,8},{8,12},{12,16},{16,20},{20,24},{24,28},{1,5},{5,9},{9,... | collective-permute-start | bytes 884744 | tf_op jit(solution)/shard_map/ppermute | solution.py:14
  16.8 6.5 %copy-start.11 = (bf16[256,2048]{1,0:T(8,128)(2,1)S(1)}, bf16[256,2048]{1,0:T(8,128)(2,1)}, u32[]{:S(2)}) copy-start(bf16[256,2048]{1,0:T(8,128)(2,1)} %param.9) | copy-start | bytes 3145732
  23.3 3.1 copy-start.19
  23.3 3.5 copy-start.14
  23.3 3.5 copy-start.12
  23.3 3.5 copy-start.17
  26.4 40.4 %copy-start.1 = (bf16[16,512,256]{2,1,0:T(8,128)(2,1)}, bf16[16,512,256]{2,1,0:T(8,128)(2,1)S(1)}, u32[]{:S(2)}) copy-start(bf16[16,512,256]{2,1,0:T(8,128)(2,1)S(1)} %convolution_convert_fusion) | copy-start | bytes 12582916
  29.0 18.2 %copy-start.6 = (f32[16,256,256]{1,2,0:T(8,128)}, f32[16,256,256]{1,2,0:T(8,128)S(1)}, u32[]{:S(2)}) copy-start(f32[16,256,256]{1,2,0:T(8,128)S(1)} %get-tuple-element.30) | copy-start | bytes 12582916
  32.3 10.9 %collective-permute-start.1 = (bf16[256,576]{0,1:T(8,128)(2,1)}, bf16[256,576]{0,1:T(8,128)(2,1)S(1)}, u32[]{:S(2)}, u32[]{:S(2)}) collective-permute-start(bf16[256,576]{0,1:T(8,128)(2,1)} %collective-permute-done), channel_id=1, source_target_pairs={{0,4},{4,8},{8,12},{12,16},{16,20},{20,24},{24,28},{1,5},{5,9},{9,... | collective-permute-start | bytes 884744 | tf_op jit(solution)/shard_map/ppermute | solution.py:14
  38.7 8.5 %copy-start.7 = (f32[16,256,256]{1,2,0:T(8,128)}, f32[16,256,256]{1,2,0:T(8,128)S(1)}, u32[]{:S(2)}) copy-start(f32[16,256,256]{1,2,0:T(8,128)S(1)} %get-tuple-element.32) | copy-start | bytes 12582916
  47.3 2.1 copy-start.15
  49.5 2.7 copy-start.4
  63.3 3.5 copy-start.3
  70.1 20.9 %copy-start.16 = (bf16[256,576]{0,1:T(8,128)(2,1)S(1)}, bf16[256,576]{0,1:T(8,128)(2,1)}, u32[]{:S(2)}) copy-start(bf16[256,576]{0,1:T(8,128)(2,1)} %param.7) | copy-start | bytes 884740
  91.0 3.4 copy-start.9
  100.4 8.5 %copy-start.10 = (bf16[256,3072]{0,1:T(8,128)(2,1)S(1)}, bf16[256,3072]{0,1:T(8,128)(2,1)}, u32[]{:S(2)}) copy-start(bf16[256,3072]{0,1:T(8,128)(2,1)} %copy.46) | copy-start | bytes 4718596
  106.7 2.2 copy-start.5
  112.1 4.3 copy-start.18
  112.2 318.0 %all-reduce.7.cloned.1.call-start = ((), (), s32[]{:S(2)}) async-start(), calls=%async_computation | async-start | bytes 1179648 | tf_op jit(solution)/shard_map/psum | solution.py:154
  112.2 13.0 %slice-start = ((s8[6291456]{0:T(1024)(128)(4,1)}), s8[4194304]{0:T(1024)(128)(4,1)S(1)}, s32[]{:S(2)}) async-start(s8[6291456]{0:T(1024)(128)(4,1)} %bitcast.137), calls=%async_computation.2 | async-start | bytes 8388608
  112.2 14.3 %slice-start.5 = ((s8[6291456]{0:T(1024)(128)(4,1)}), s8[4194304]{0:T(1024)(128)(4,1)S(1)}, s32[]{:S(2)}) async-start(s8[6291456]{0:T(1024)(128)(4,1)} %bitcast.141), calls=%async_computation.7 | async-start | bytes 8388608
  116.5 8.7 %copy-start.2 = (bf16[16,512,256]{2,1,0:T(8,128)(2,1)S(1)}, bf16[16,512,256]{2,1,0:T(8,128)(2,1)}, u32[]{:S(2)}) copy-start(bf16[16,512,256]{2,1,0:T(8,128)(2,1)} %copy-done.1) | copy-start | bytes 12582916
  116.5 8.7 %slice-start.1 = ((s8[6291456]{0:T(1024)(128)(4,1)}), s8[2097152]{0:T(1024)(128)(4,1)S(1)}, s32[]{:S(2)}) async-start(s8[6291456]{0:T(1024)(128)(4,1)} %bitcast.137), calls=%async_computation.3 | async-start | bytes 4194304
  116.5 10.0 %slice-start.6 = ((s8[6291456]{0:T(1024)(128)(4,1)}), s8[2097152]{0:T(1024)(128)(4,1)S(1)}, s32[]{:S(2)}) async-start(s8[6291456]{0:T(1024)(128)(4,1)} %bitcast.141), calls=%async_computation.8 | async-start | bytes 4194304
  121.7 4.9 %copy-start.13 = (bf16[256,16,512]{0,2,1:T(8,128)(2,1)S(1)}, bf16[256,16,512]{0,2,1:T(8,128)(2,1)}, u32[]{:S(2)}) copy-start(bf16[256,16,512]{0,2,1:T(8,128)(2,1)} %convert_bitcast_fusion) | copy-start | bytes 12582916
  121.7 23.0 %collective-permute-start.2 = (bf16[256,576]{0,1:T(8,128)(2,1)S(1)}, bf16[256,576]{0,1:T(8,128)(2,1)S(1)}, u32[]{:S(2)}, u32[]{:S(2)}) collective-permute-start(bf16[256,576]{0,1:T(8,128)(2,1)S(1)} %fusion.95), channel_id=1, source_target_pairs={{4,0},{8,4},{12,8},{16,12},{20,16},{24,20},{28,24},{5,1},{9,5},{13... | collective-permute-start | bytes 884744 | tf_op jit(solution)/shard_map/ppermute | solution.py:14
  125.2 6.0 %slice-start.2 = ((s8[4718592]{0:T(1024)(128)(4,1)}), s8[4194304]{0:T(1024)(128)(4,1)S(1)}, s32[]{:S(2)}) async-start(s8[4718592]{0:T(1024)(128)(4,1)} %bitcast.139), calls=%async_computation.4 | async-start | bytes 8388608
  126.5 4.7 %slice-start.3 = ((s8[4718592]{0:T(1024)(128)(4,1)}), s8[524288]{0:T(1024)(128)(4,1)S(1)}, s32[]{:S(2)}) async-start(s8[4718592]{0:T(1024)(128)(4,1)} %bitcast.139), calls=%async_computation.5 | async-start | bytes 1048576
  128.0 24.8 %collective-permute-start.3 = (bf16[256,576]{0,1:T(8,128)(2,1)S(1)}, bf16[256,576]{0,1:T(8,128)(2,1)S(1)}, u32[]{:S(2)}, u32[]{:S(2)}) collective-permute-start(bf16[256,576]{0,1:T(8,128)(2,1)S(1)} %fusion.98), channel_id=1, source_target_pairs={{8,0},{12,4},{16,8},{20,12},{24,16},{28,20},{9,1},{13,5},{17,9},{2... | collective-permute-start | bytes 884744 | tf_op jit(solution)/shard_map/ppermute | solution.py:14
  155.0 7.7 %slice-start.4 = ((bf16[256,16,576]{0,2,1:T(8,128)(2,1)}), bf16[256,16,64]{0,2,1:T(8,128)(2,1)S(1)}, s32[]{:S(2)}) async-start(bf16[256,16,576]{0,2,1:T(8,128)(2,1)} %copy-done.5), calls=%async_computation.6 | async-start | bytes 1048576 | tf_op jit(solution)/shard_map/slice | solution.py:147
  (1 other events, 2.0 us)
Sparse Core Ops, SparseCore 0:
  112.3 281.5 all-reduce.8
  396.8 33.2 all-reduce.6
where the time goes:
time: 442 us; the launch traced here: 439 us
  waiting for transfers between devices  271 us (61%)
  matrix products  83.2 us (19%)
  other arithmetic  27.7 us (6%)
  local copies, waits for them, and re-layouts  27.6 us (6%)
  between operations  16.5 us (4%)
  starting transfers between devices  12.5 us (3%)
    psum x1, waiting for transfers between devices, body(): d_w_uk, d_w_uv = lax.psum((grad_uk, grad_uv), 'ctx')  226 us
    psum x1, waiting for transfers between devices, body(): d_latent = lax.psum(key_parts[0] + returned, 'head')  25.6 us
    unnamed x58, local copies, waits for them, and re-layouts  24.2 us
    sub x1, other arithmetic, body(): d_scores = (probs * (d_probs - delta) * inv_root).astype(jnp.bfloat16)  20.8 us
    ppermute x4, waiting for transfers between devices, shifted(): return lax.ppermute(block, axis, route)  19.8 us
    dot_general x3, matrix products, dquery_fn(): jnp.einsum('htk,kl->thl', block_grads, block_keys, preferred_element_type...  15.4 us
    dot_general x3, matrix products, value_fn(): jnp.einsum('htk,kr->thr', block_probs, block_keys[:, :rank_width], prefer...  12.4 us
    ppermute x4, starting transfers between devices, shifted(): return lax.ppermute(block, axis, route)  12.4 us
  transfers between devices with their start and end apart: 6, of which 4 were waited for; matrix products, arithmetic and copies ran while one was open for 15% of the time, Pallas kernels for 0%

commit v1 on v0

v1 whole, which is shorter than its diff:
```python
import functools
import math

import jax
import jax.numpy as jnp
from jax import lax
from jax.experimental import pallas as pl
from jax.experimental.pallas import tpu as pltpu
from jax.sharding import PartitionSpec as P

SPAN = 2
PAIR = 2
CHUNKS = 4


def dot(a, b):
    return lax.dot_general(a, b, (((1,), (0,)), ((), ())), preferred_element_type=jnp.float32)


def dot_t(a, b):
    return lax.dot_general(a, b, (((1,), (1,)), ((), ())), preferred_element_type=jnp.float32)


def attention_kernel(
    nope, rope, rank, value,
    keys_ref, keys_t_ref, bias_ref, query_ref, grads_ref, uk_ref, uv_ref, *rest,
):
    att_ref, dq_ref, dkeys_ref, duk_ref, duv_ref = rest[-5:]
    bf16 = jnp.bfloat16
    width = nope + rope
    inv_root = 1.0 / math.sqrt(width)
    to_log2 = inv_root * math.log2(math.e)

    @pl.when(pl.program_id(0) == 0)
    def _():
        dkeys_ref[...] = jnp.zeros_like(dkeys_ref)

    queries = query_ref[...]
    for head in range(PAIR):
        q_nope = queries[:, head * width : head * width + nope]
        q_rope = queries[:, head * width + nope : (head + 1) * width]
        grads = grads_ref[:, head * value : (head + 1) * value]
        w_uk = uk_ref[head]
        w_uv = uv_ref[head]
        absorbed = dot(q_nope, w_uk).astype(bf16)
        d_out_latent = dot(grads, w_uv).astype(bf16)
        content = keys_ref[:, :rank]
        scores = dot_t(content, absorbed) + dot_t(keys_ref[:, rank:], q_rope)
        scores = scores * to_log2 + bias_ref[...]
        weights = jnp.exp2(scores - jnp.max(scores, axis=0, keepdims=True))
        probs = weights * (1.0 / jnp.sum(weights, axis=0, keepdims=True))
        low = probs.astype(bf16)
        out_t = dot(keys_t_ref[:rank, :], low).astype(bf16)
        att_t = dot(w_uv, out_t)
        att_ref[:, head * value : (head + 1) * value] = att_t.T.astype(bf16)
        duv_ref[head] = dot_t(grads.T, out_t).astype(duv_ref.dtype)
        d_probs = dot_t(content, d_out_latent)
        delta = jnp.sum(probs * d_probs, axis=0, keepdims=True)
        d_scores = (probs * (d_probs - delta) * inv_root).astype(bf16)
        d_full_t = dot(keys_t_ref[...], d_scores)
        d_absorbed_t = d_full_t[:rank].astype(bf16)
        d_nope_t = dot(w_uk, d_absorbed_t)
        dq_ref[:, head * width : (head + 1) * width] = jnp.concatenate(
            [d_nope_t, d_full_t[rank:]], axis=0
        ).T.astype(bf16)
        duk_ref[head] = dot_t(q_nope.T, d_absorbed_t).astype(duk_ref.dtype)
        dkeys_ref[:, :rank] += dot(d_scores, absorbed) + dot(low, d_out_latent)
        dkeys_ref[:, rank:] += dot(d_scores, q_rope)


def attend(chunk, chunks, keys, keys_t, bias, query, d_out, w_uk, w_uv, *filled):
    tok = query.shape[0]
    heads, nope, rank = w_uk.shape
    value = w_uv.shape[1]
    width = query.shape[1] // heads
    lat = keys.shape[1]
    span = keys.shape[0]
    steps = heads // chunks // PAIR
    first = chunk * steps
    fixed = lambda i: (0, 0)
    columns = lambda i: (0, first + i)
    weight = lambda i: (first + i, 0, 0)
    own = lambda i: (i, 0, 0)
    here = steps * PAIR
    flops = 2 * tok * here * (span * (3 * lat + 3 * rank) + 6 * nope * rank)
    return pl.pallas_call(
        functools.partial(attention_kernel, nope, width - nope, rank, value),
        grid=(steps,),
        in_specs=[
            pl.BlockSpec((span, lat), fixed),
            pl.BlockSpec((lat, span), fixed),
            pl.BlockSpec((span, tok), fixed),
            pl.BlockSpec((tok, PAIR * width), columns),
            pl.BlockSpec((tok, PAIR * value), columns),
            pl.BlockSpec((PAIR, nope, rank), weight),
            pl.BlockSpec((PAIR, value, rank), weight),
        ]
        + [pl.BlockSpec(memory_space=pl.ANY) for _ in filled],
        out_specs=[
            pl.BlockSpec((tok, PAIR * value), columns),
            pl.BlockSpec((tok, PAIR * width), columns),
            pl.BlockSpec((span, lat), fixed),
            pl.BlockSpec((PAIR, nope, rank), own),
            pl.BlockSpec((PAIR, value, rank), own),
        ],
        out_shape=[
            jax.ShapeDtypeStruct((tok, heads * value), jnp.bfloat16),
            jax.ShapeDtypeStruct((tok, heads * width), jnp.bfloat16),
            jax.ShapeDtypeStruct((span, lat), jnp.float32),
            jax.ShapeDtypeStruct((here, nope, rank), jnp.bfloat16),
            jax.ShapeDtypeStruct((here, value, rank), jnp.bfloat16),
        ],
        input_output_aliases={7 + i: i for i in range(len(filled))},
        compiler_params=pltpu.CompilerParams(vmem_limit_bytes=48 * 1024 * 1024),
        cost_estimate=pl.CostEstimate(
            flops=flops, bytes_accessed=8 * span * lat, transcendentals=tok * here * span
        ),
    )(keys, keys_t, bias, query, d_out, w_uk, w_uv, *filled)


def shifted(block, axis, distance):
    devices = range(lax.axis_size(axis))
    route = [(i - distance, i) for i in devices if i - distance in devices]
    return lax.ppermute(block, axis, route)


def mask_bias(tok, block_mask, segments):
    position = lax.axis_index("ctx")
    offsets = jnp.arange(tok, dtype=jnp.int32)
    seg_query = lax.dynamic_slice_in_dim(segments, position * tok, tok)
    parts = []
    for back in range(SPAN + 1):
        block = position - back
        clamped = jnp.maximum(block, 0)
        seg_key = lax.dynamic_slice_in_dim(segments, clamped * tok, tok)
        granted = block_mask[position, clamped] == 1
        allowed = (block >= 0) & ((seg_query[None, :] == seg_key[:, None]) | granted)
        if back == 0:
            allowed = allowed & (offsets[:, None] <= offsets[None, :])
        parts.append(jnp.where(allowed, 0.0, -jnp.inf).astype(jnp.float32))
    return jnp.concatenate(parts, axis=0)


def body(latent, query, d_out, w_uk, w_uv, block_mask, segments):
    tok = latent.shape[0]
    heads = w_uk.shape[0]
    chunks = CHUNKS
    bias = mask_bias(tok, block_mask, segments)
    keys = jnp.concatenate([latent] + [shifted(latent, "ctx", d) for d in range(1, SPAN + 1)], axis=0)
    keys_t = keys.T
    filled = ()
    d_keys = None
    uk_parts, uv_parts = [], []
    for chunk in range(chunks):
        att, dq, part, uk, uv = attend(
            chunk, chunks, keys, keys_t, bias, query, d_out, w_uk, w_uv, *filled
        )
        filled = (att, dq)
        d_keys = part if d_keys is None else d_keys + part
        if uk_parts:
            uk, uv, uk_parts[-1], uv_parts[-1] = lax.optimization_barrier(
                (uk, uv, uk_parts[-1], uv_parts[-1])
            )
        uk, uv = lax.psum((uk, uv), "ctx")
        uk_parts.append(uk)
        uv_parts.append(uv)
    d_keys = d_keys.astype(jnp.bfloat16).reshape(SPAN + 1, tok, -1)
    shares = lax.psum_scatter(d_keys, "head", scatter_dimension=1, tiled=True)
    total = shares[0].astype(jnp.float32)
    for back in range(1, SPAN + 1):
        total = total + shifted(shares[back], "ctx", -back).astype(jnp.float32)
    d_latent = lax.all_gather(total.astype(jnp.bfloat16), "head", axis=0, tiled=True)
    d_w_uk = jnp.concatenate(uk_parts, axis=0).astype(jnp.float32)
    d_w_uv = jnp.concatenate(uv_parts, axis=0).astype(jnp.float32)
    return att, dq, d_latent.astype(jnp.float32), d_w_uk, d_w_uv


def solution(mesh):
    in_specs = (
        P("ctx", None),
        P("ctx", "head"),
        P("ctx", "head"),
        P("head", None, None),
        P("head", None, None),
        P(),
        P(),
    )
    out_specs = (
        P("ctx", "head"),
        P("ctx", "head"),
        P("ctx", None),
        P("head", None, None),
        P("head", None, None),
    )
    return jax.shard_map(body, mesh=mesh, in_specs=in_specs, out_specs=out_specs, check_vma=False)
```

time: 442 us -> 421 us (0.952)
  matrix products: 83.2 us -> 0 us
  Pallas kernels: 0 us -> 60.2 us
  waiting for transfers between devices: 271 us -> 302 us
  other arithmetic: 27.7 us -> 6.94 us
  local copies, waits for them, and re-layouts: 27.6 us -> 14 us
  blocking collectives: 0 us -> 6.18 us
    dot_general x24 -> x0, matrix products: 83.2 us -> none  [the longest x3 15.4 us: dquery_fn(): jnp.einsum('htk,kl->thl', block_grads, block_keys, preferred_element_type...]
    pallas_call x0 -> x4, Pallas kernels: none -> 60.2 us  [attend(): pl.pallas_call(functools.partial(attention_kernel, nope, width - nope, ra...]
    unnamed x2 -> x6, waiting for transfers between devices: 0.03 us -> 39.4 us
    sub x1 -> x0, other arithmetic: 20.8 us -> none  [body(): d_scores = (probs * (d_probs - delta) * inv_root).astype(jnp.bfloat16)]
    unnamed x58 -> x34, local copies, waits for them, and re-layouts: 24.2 us -> 7.51 us
    ppermute x4, waiting for transfers between devices: 19.8 us -> 9.44 us  [shifted(): return lax.ppermute(block, axis, route)]
    all_gather x0 -> x1, blocking collectives: none -> 6.18 us  [body(): lax.all_gather(total.astype(jnp.bfloat16), 'head', axis=0, tiled=True)]
    convert_element_type x1 -> x3, other arithmetic: 2.14 us -> 6.67 us  [the longest x1 4.72 us: body(): d_w_uk = jnp.concatenate(uk_parts, axis=0).astype(jnp.float32)]
  transfers between devices with their start and end apart: 6 -> 9, of which waited for: 4 -> 8; matrix products, arithmetic and copies ran while one was open for 15% -> 3% of each run, Pallas kernels for 0% -> 11%
where the time goes in v1:
time: 421 us; the launch traced here: 419 us
  waiting for transfers between devices  302 us (72%)
  Pallas kernels  60.2 us (14%)
  between operations  16.9 us (4%)
  local copies, waits for them, and re-layouts  14 us (3%)
  starting transfers between devices  12.1 us (3%)
  other arithmetic  6.94 us (2%)
  blocking collectives  6.18 us (1%)
    psum x4, waiting for transfers between devices, body(): uk, uv = lax.psum((uk, uv), 'ctx')  254 us
    pallas_call x4, Pallas kernels, attend(): pl.pallas_call(functools.partial(attention_kernel, nope, width - nope, ra...  60.2 us
    unnamed x6, waiting for transfers between devices  39.4 us
    ppermute x4, starting transfers between devices, shifted(): return lax.ppermute(block, axis, route)  11.8 us
    ppermute x4, waiting for transfers between devices, shifted(): return lax.ppermute(block, axis, route)  9.44 us
  transfers between devices with their start and end apart: 9, of which 8 were waited for; matrix products, arithmetic and copies ran while one was open for 3% of the time, Pallas kernels for 11%

profile of v1, /device:TPU:14, one launch (start us, length us, event | category | flops | bytes accessed | tf_op | source)
XLA Modules:
  0.0 418.8 jit_solution(16983854407275800763)
XLA Ops:
  7.2 3.5 collective-permute-start
  10.7 3.5 collective-permute-start.1
  14.2 1.4 fusion.5
  17.5 0.9 fusion.4
  18.5 0.2 fusion.1
  18.7 1.0 constant_dynamic-update-slice_fusion.2
  19.8 4.6 %collective-permute-done.1 = bf16[256,576]{0,1:T(8,128)(2,1)S(1)} collective-permute-done((bf16[256,576]{0,1:T(8,128)(2,1)}, bf16[256,576]{0,1:T(8,128)(2,1)S(1)}, u32[]{:S(2)}, u32[]{:S(2)}) %collective-permute-start.1) | collective-permute-done | bytes 294944 | tf_op jit(solution)/shard_map/ppermute | solution.py:124
  24.4 0.6 copy.34.keys_ref
  25.0 1.2 copy-done
  26.2 15.0 %shard_map.110 = (bf16[256,2048]{1,0:T(8,128)(2,1)}, bf16[256,3072]{1,0:T(8,128)(2,1)}, f32[768,576]{1,0:T(8,128)}, bf16[4,128,512]{2,1,0:T(8,128)(2,1)}, bf16[4,128,512]{2,1,0:T(8,128)(2,1)}) custom-call(bf16[768,576]{1,0:T(8,128)(2,1)S(1)} %copy.34.keys_ref, bf16[576,768]{1,0:T(8,128)(2,1)S(1)} %bitcast.17, f32[768,256]{1,0:T(8,128)S(1)} %pad_maximum_fusion.bias_ref, ...), custom_call_target="tpu_custom_call" | custom-call | flops 5939134464 | bytes 3538944 | tf_op jit(solution)/shard_map/pallas_call | solution.py:86
  41.3 1.2 copy-done.1
  42.5 15.0 %shard_map.111 = (bf16[256,2048]{1,0:T(8,128)(2,1)}, bf16[256,3072]{1,0:T(8,128)(2,1)}, f32[768,576]{1,0:T(8,128)}, bf16[4,128,512]{2,1,0:T(8,128)(2,1)}, bf16[4,128,512]{2,1,0:T(8,128)(2,1)}) custom-call(bf16[768,576]{1,0:T(8,128)(2,1)S(1)} %copy.34.keys_ref, bf16[576,768]{1,0:T(8,128)(2,1)S(1)} %bitcast.18, ...), custom_call_target="tpu_custom_call", output_to_operand_aliasing={{0}: (7, {}), {1}: (8, {})} | custom-call | flops 5939134464 | bytes 3538944 | tf_op jit(solution)/shard_map/pallas_call | solution.py:86
  57.6 62.9 %all-reduce.19.cloned.1.call-done = (bf16[4,128,512]{2,1,0:T(8,128)(2,1)}, bf16[4,128,512]{2,1,0:T(8,128)(2,1)}) async-done(((bf16[4,128,512]{2,1,0:T(8,128)(2,1)}, bf16[4,128,512]{2,1,0:T(8,128)(2,1)}), (bf16[4,128,512]{2,1,0:T(8,128)(2,1)}, bf16[4,128,512]{2,1,0:T(8,128)(2,1)})) %all-reduce.19.cloned.1.call-update) | async-done | bytes 1048592 | tf_op jit(solution)/shard_map/psum | solution.py:164
  120.7 1.2 copy-done.2
  122.0 15.0 %shard_map.112 = (bf16[256,2048]{1,0:T(8,128)(2,1)}, bf16[256,3072]{1,0:T(8,128)(2,1)}, f32[768,576]{1,0:T(8,128)}, bf16[4,128,512]{2,1,0:T(8,128)(2,1)}, bf16[4,128,512]{2,1,0:T(8,128)(2,1)}) custom-call(bf16[768,576]{1,0:T(8,128)(2,1)S(1)} %copy.34.keys_ref, bf16[576,768]{1,0:T(8,128)(2,1)S(1)} %bitcast.19, ...), custom_call_target="tpu_custom_call", output_to_operand_aliasing={{0}: (7, {}), {1}: (8, {})} | custom-call | flops 5939134464 | bytes 3538944 | tf_op jit(solution)/shard_map/pallas_call | solution.py:86
  137.0 65.2 %all-reduce.17.cloned.1.call-done = (bf16[4,128,512]{2,1,0:T(8,128)(2,1)}, bf16[4,128,512]{2,1,0:T(8,128)(2,1)}) async-done(((bf16[4,128,512]{2,1,0:T(8,128)(2,1)}, bf16[4,128,512]{2,1,0:T(8,128)(2,1)}), (bf16[4,128,512]{2,1,0:T(8,128)(2,1)}, bf16[4,128,512]{2,1,0:T(8,128)(2,1)})) %all-reduce.17.cloned.1.call-update) | async-done | bytes 1048592 | tf_op jit(solution)/shard_map/psum | solution.py:164
  202.2 1.2 copy-done.3
  203.4 15.2 %shard_map.113 = (bf16[256,2048]{1,0:T(8,128)(2,1)}, bf16[256,3072]{1,0:T(8,128)(2,1)}, f32[768,576]{1,0:T(8,128)}, bf16[4,128,512]{2,1,0:T(8,128)(2,1)}, bf16[4,128,512]{2,1,0:T(8,128)(2,1)}) custom-call(bf16[768,576]{1,0:T(8,128)(2,1)S(1)} %copy.34.keys_ref, bf16[576,768]{1,0:T(8,128)(2,1)S(1)} %bitcast.20, ...), custom_call_target="tpu_custom_call", output_to_operand_aliasing={{0}: (7, {}), {1}: (8, {})} | custom-call | flops 5939134464 | bytes 3538944 | tf_op jit(solution)/shard_map/pallas_call | solution.py:86
  218.7 1.9 add_convert_fusion
  220.6 1.9 copy.35
  222.6 61.6 %all-reduce.15.cloned.1.call-done = (bf16[4,128,512]{2,1,0:T(8,128)(2,1)}, bf16[4,128,512]{2,1,0:T(8,128)(2,1)}) async-done(((bf16[4,128,512]{2,1,0:T(8,128)(2,1)}, bf16[4,128,512]{2,1,0:T(8,128)(2,1)}), (bf16[4,128,512]{2,1,0:T(8,128)(2,1)}, bf16[4,128,512]{2,1,0:T(8,128)(2,1)})) %all-reduce.15.cloned.1.call-update) | async-done | bytes 1048592 | tf_op jit(solution)/shard_map/psum | solution.py:164
  284.2 0.6 dynamic-slice
  285.7 39.3 %all-reduce.11.cloned.1.call-done = bf16[3,256,576]{2,0,1:T(4,128)(2,1)} async-done(((bf16[3,256,576]{2,0,1:T(4,128)(2,1)}), bf16[3,256,576]{2,0,1:T(4,128)(2,1)}) %all-reduce.11.cloned.1.call-update) | async-done | bytes 884752
  325.0 1.6 constant_dynamic-slice_fusion.1
  326.6 2.4 collective-permute-start.3
  329.1 2.4 collective-permute-start.2
  331.5 1.5 collective-permute-done.3
  333.0 3.4 collective-permute-done.2
  336.4 6.2 %all_gather.3 = bf16[256,576]{1,0:T(8,128)(2,1)S(1)} all-gather(bf16[64,576]{1,0:T(8,128)(2,1)S(1)} %fusion.3), channel_id=1, replica_groups=mesh['ctx'=8,'head'=4] {'head'}, dimensions={0}, use_global_device_ids=true | all-gather | bytes 368640 | tf_op jit(solution)/shard_map/all_gather | solution.py:172
  342.6 1.0 copy.39
  343.5 63.9 %all-reduce.13.cloned.1.call-done = (bf16[4,128,512]{2,1,0:T(8,128)(2,1)}, bf16[4,128,512]{2,1,0:T(8,128)(2,1)}) async-done(((bf16[4,128,512]{2,1,0:T(8,128)(2,1)}, bf16[4,128,512]{2,1,0:T(8,128)(2,1)}), (bf16[4,128,512]{2,1,0:T(8,128)(2,1)}, bf16[4,128,512]{2,1,0:T(8,128)(2,1)})) %all-reduce.13.cloned.1.call-update) | async-done | bytes 1048592 | tf_op jit(solution)/shard_map/psum | solution.py:164
  407.5 4.7 %maximum_convert_fusion = (f32[16,128,512]{2,1,0:T(8,128)}, f32[16,128,512]{2,1,0:T(8,128)}) fusion(bf16[4,128,512]{2,1,0:T(8,128)(2,1)} %get-tuple-element.79, bf16[4,128,512]{2,1,0:T(8,128)(2,1)S(1)} %copy-done.11, bf16[4,128,512]{2,1,0:T(8,128)(2,1)S(1)} %copy-done.9, bf16[4,128,512]{2,1,0:T(8,128)(2,1)S(1)} %copy-done.7, ...), kind=kLoop, calls=%fused_computation | loop fusion | flops 8388608 | bytes 12582912 | tf_op jit(solution)/shard_map/convert_element_type | solution.py:173
  (41 shorter events, 0.7 us)
Async XLA Ops:
  7.2 113.3 %all-reduce.19.cloned.1.call-start = ((), (), s32[]{:S(2)}) async-start(), calls=%async_computation.4 | async-start | bytes 2097152 | tf_op jit(solution)/shard_map/psum | solution.py:164
  7.2 12.5 %collective-permute-start = (bf16[256,576]{0,1:T(8,128)(2,1)}, bf16[256,576]{0,1:T(8,128)(2,1)S(1)}, u32[]{:S(2)}, u32[]{:S(2)}) collective-permute-start(bf16[256,576]{0,1:T(8,128)(2,1)} %param.7), channel_id=1, source_target_pairs={{0,4},{4,8},{8,12},{12,16},{16,20},{20,24},{24,28},{1,5},{5,9},{9,... | collective-permute-start | bytes 884744 | tf_op jit(solution)/shard_map/ppermute | solution.py:124
  10.7 13.7 %collective-permute-start.1 = (bf16[256,576]{0,1:T(8,128)(2,1)}, bf16[256,576]{0,1:T(8,128)(2,1)S(1)}, u32[]{:S(2)}, u32[]{:S(2)}) collective-permute-start(bf16[256,576]{0,1:T(8,128)(2,1)} %param.7), channel_id=1, source_target_pairs={{0,8},{4,12},{8,16},{12,20},{16,24},{20,28},{1,9},{5,13},{9,17},{1... | collective-permute-start | bytes 884744 | tf_op jit(solution)/shard_map/ppermute | solution.py:124
  25.0 1.2 copy-start
  41.3 160.9 %all-reduce.17.cloned.1.call-start = ((), (), s32[]{:S(2)}) async-start(), calls=%async_computation.3 | async-start | bytes 2097152 | tf_op jit(solution)/shard_map/psum | solution.py:164
  41.3 1.2 copy-start.1
  120.5 163.6 %all-reduce.15.cloned.1.call-start = ((), (), s32[]{:S(2)}) async-start(), calls=%async_computation.2 | async-start | bytes 2097152 | tf_op jit(solution)/shard_map/psum | solution.py:164
  120.7 1.2 copy-start.2
  202.2 122.8 %all-reduce.11.cloned.1.call-start = ((), (), s32[]{:S(2)}) async-start(), calls=%async_computation | async-start | bytes 2621440
  202.2 1.2 copy-start.3
  203.4 15.2 %copy-start.4 = (f32[768,576]{1,0:T(8,128)S(1)}, f32[768,576]{1,0:T(8,128)}, u32[]{:S(2)}) copy-start(f32[768,576]{1,0:T(8,128)} %get-tuple-element.45) | copy-start | bytes 5308420
  203.4 15.2 %copy-start.5 = (f32[768,576]{1,0:T(8,128)S(1)}, f32[768,576]{1,0:T(8,128)}, u32[]{:S(2)}) copy-start(f32[768,576]{1,0:T(8,128)} %get-tuple-element.46) | copy-start | bytes 5308420
  203.4 15.2 %copy-start.6 = (f32[768,576]{1,0:T(8,128)S(1)}, f32[768,576]{1,0:T(8,128)}, u32[]{:S(2)}) copy-start(f32[768,576]{1,0:T(8,128)} %get-tuple-element.47) | copy-start | bytes 5308420
  220.6 63.6 %copy-start.13 = (u32[32]{0:T(128)S(1)}, u32[32]{0:T(128)}, u32[]{:S(2)}) copy-start(u32[32]{0:T(128)} %constant.33) | copy-start | bytes 388
  222.5 185.0 %all-reduce.13.cloned.1.call-start = ((), (), s32[]{:S(2)}) async-start(), calls=%async_computation.1 | async-start | bytes 2097152 | tf_op jit(solution)/shard_map/psum | solution.py:164
  284.1 123.4 %copy-start.7 = (bf16[4,128,512]{2,1,0:T(8,128)(2,1)S(1)}, bf16[4,128,512]{2,1,0:T(8,128)(2,1)}, u32[]{:S(2)}) copy-start(bf16[4,128,512]{2,1,0:T(8,128)(2,1)} %get-tuple-element.53) | copy-start | bytes 1572868
  284.1 123.4 %copy-start.8 = (bf16[4,128,512]{2,1,0:T(8,128)(2,1)S(1)}, bf16[4,128,512]{2,1,0:T(8,128)(2,1)}, u32[]{:S(2)}) copy-start(bf16[4,128,512]{2,1,0:T(8,128)(2,1)} %get-tuple-element.65) | copy-start | bytes 1572868
  284.1 123.4 %copy-start.9 = (bf16[4,128,512]{2,1,0:T(8,128)(2,1)S(1)}, bf16[4,128,512]{2,1,0:T(8,128)(2,1)}, u32[]{:S(2)}) copy-start(bf16[4,128,512]{2,1,0:T(8,128)(2,1)} %get-tuple-element.58) | copy-start | bytes 1572868
  284.1 123.4 %copy-start.10 = (bf16[4,128,512]{2,1,0:T(8,128)(2,1)S(1)}, bf16[4,128,512]{2,1,0:T(8,128)(2,1)}, u32[]{:S(2)}) copy-start(bf16[4,128,512]{2,1,0:T(8,128)(2,1)} %get-tuple-element.66) | copy-start | bytes 1572868
  284.1 123.4 %copy-start.11 = (bf16[4,128,512]{2,1,0:T(8,128)(2,1)S(1)}, bf16[4,128,512]{2,1,0:T(8,128)(2,1)}, u32[]{:S(2)}) copy-start(bf16[4,128,512]{2,1,0:T(8,128)(2,1)} %get-tuple-element.63) | copy-start | bytes 1572868
  284.1 123.4 %copy-start.12 = (bf16[4,128,512]{2,1,0:T(8,128)(2,1)S(1)}, bf16[4,128,512]{2,1,0:T(8,128)(2,1)}, u32[]{:S(2)}) copy-start(bf16[4,128,512]{2,1,0:T(8,128)(2,1)} %get-tuple-element.67) | copy-start | bytes 1572868
  326.6 6.3 %collective-permute-start.3 = (bf16[64,576]{1,0:T(8,128)(2,1)S(1)}, bf16[64,576]{1,0:T(8,128)(2,1)S(1)}, u32[]{:S(2)}, u32[]{:S(2)}) collective-permute-start(bf16[64,576]{1,0:T(8,128)(2,1)S(1)} %bitcast.22), channel_id=1, source_target_pairs={{8,0},{12,4},{16,8},{20,12},{24,16},{28,20},{9,1},{13,5},{17,9},{2... | collective-permute-start | bytes 221192 | tf_op jit(solution)/shard_map/ppermute | solution.py:124
  329.1 7.2 %collective-permute-start.2 = (bf16[64,576]{1,0:T(8,128)(2,1)S(1)}, bf16[64,576]{1,0:T(8,128)(2,1)S(1)}, u32[]{:S(2)}, u32[]{:S(2)}) collective-permute-start(bf16[64,576]{1,0:T(8,128)(2,1)S(1)} %bitcast.23), channel_id=1, source_target_pairs={{4,0},{8,4},{12,8},{16,12},{20,16},{24,20},{28,24},{5,1},{9,5},{13... | collective-permute-start | bytes 221192 | tf_op jit(solution)/shard_map/ppermute | solution.py:124
Sparse Core Ops, SparseCore 0:
  41.4 79.0 all-reduce.18
  124.4 77.6 all-reduce.16
  206.3 77.8 all-reduce.14
  287.0 37.8 all-reduce.10
  328.8 78.6 all-reduce.12

commit v2 on v1

v2 whole, which is shorter than its diff:
```python
import functools
import math

import jax
import jax.numpy as jnp
from jax import lax
from jax.experimental import pallas as pl
from jax.experimental.pallas import tpu as pltpu
from jax.sharding import PartitionSpec as P

SPAN = 2
PAIR = 2
LAGS = (1, 2, 4, 6)


def dot(a, b):
    return lax.dot_general(a, b, (((1,), (0,)), ((), ())), preferred_element_type=jnp.float32)


def dot_t(a, b):
    return lax.dot_general(a, b, (((1,), (1,)), ((), ())), preferred_element_type=jnp.float32)


def attention_kernel(
    nope, rope, rank, value, steps, n, peers,
    keys_ref, keys_t_ref, bias_ref, query_ref, grads_ref, uk_ref, uv_ref,
    att_ref, dq_ref, dlat_ref, duk_ref, duv_ref,
    dkeys, own, from_pair, mid, from_line, final, sent, from_head, shifts, from_ctx, gathered,
    pair_send, pair_recv, line_send, line_recv, back_send, back_recv, last_send, last_recv,
    head_send, head_recv, ctx_send, ctx_recv, out_send, out_recv,
):
    bf16, f32 = jnp.bfloat16, jnp.float32
    width = nope + rope
    inv_root = 1.0 / math.sqrt(width)
    to_log2 = inv_root * math.log2(math.e)
    step = pl.program_id(0)
    me = lax.axis_index("ctx")
    head_me = lax.axis_index("head")
    parity = lax.rem(me, 2)
    place = me // 2
    line = n // 2
    half = own.shape[1] // 2
    part = half // line
    tok = att_ref.shape[0]
    quarter = tok // peers

    def remote(src, dst, send, recv, target):
        return pltpu.make_async_remote_copy(
            src_ref=src, dst_ref=dst, send_sem=send, recv_sem=recv,
            device_id=target, device_id_type=pl.DeviceIdType.MESH,
        )

    def half_rows(which):
        return pl.ds(pl.multiple_of(which * half, 16), half)

    def part_rows(at):
        return pl.ds(pl.multiple_of(at * part, 16), part)

    def pair_copy(c):
        return remote(
            own.at[c, half_rows(1 - parity)], from_pair.at[c],
            pair_send.at[c], pair_recv.at[c], {"ctx": me + 1 - 2 * parity},
        )

    def line_copy(c, d):
        peer = lax.rem(place + d, line)
        return remote(
            mid.at[c, part_rows(peer)], from_line.at[c, d - 1],
            line_send.at[c, d - 1], line_recv.at[c, d - 1], {"ctx": peer * 2 + parity},
        )

    def back_copy(c, d):
        peer = lax.rem(place + d, line)
        rows = pl.ds(pl.multiple_of(parity * half + place * part, 16), part)
        return remote(
            final.at[c, rows], final.at[c, rows],
            back_send.at[c, d - 1], back_recv.at[c, d - 1], {"ctx": peer * 2 + parity},
        )

    def last_copy(c):
        rows = half_rows(parity)
        return remote(
            final.at[c, rows], final.at[c, rows],
            last_send.at[c], last_recv.at[c], {"ctx": me + 1 - 2 * parity},
        )

    def head_copy(d):
        peer = lax.rem(head_me + d, peers)
        rows = pl.ds(pl.multiple_of(peer * quarter, 16), quarter)
        return remote(
            sent.at[:, rows, :], from_head.at[d - 1],
            head_send.at[d - 1], head_recv.at[d - 1], {"head": peer},
        )

    def ctx_copy(d):
        return remote(
            shifts.at[d - 1], from_ctx.at[d - 1],
            ctx_send.at[d - 1], ctx_recv.at[d - 1], {"ctx": lax.rem(me - d + n, n)},
        )

    def out_copy(d):
        peer = lax.rem(head_me + d, peers)
        rows = pl.ds(pl.multiple_of(head_me * quarter, 16), quarter)
        return remote(
            gathered.at[rows], gathered.at[rows],
            out_send.at[d - 1], out_recv.at[d - 1], {"head": peer},
        )

    @pl.when(step == 0)
    def _():
        dkeys[...] = jnp.zeros_like(dkeys)
        barrier = pltpu.get_barrier_semaphore()
        for d in range(1, n):
            pl.semaphore_signal(
                barrier, inc=1, device_id={"ctx": lax.rem(me + d, n)},
                device_id_type=pl.DeviceIdType.MESH,
            )
        for d in range(1, peers):
            pl.semaphore_signal(
                barrier, inc=1, device_id={"head": lax.rem(head_me + d, peers)},
                device_id_type=pl.DeviceIdType.MESH,
            )
        pl.semaphore_wait(barrier, n - 1 + peers - 1)

    @pl.when(step < steps)
    def _():
        queries = query_ref[...]
        for head in range(PAIR):
            q_nope = queries[:, head * width : head * width + nope]
            q_rope = queries[:, head * width + nope : (head + 1) * width]
            grads = grads_ref[:, head * value : (head + 1) * value]
            w_uk = uk_ref[head]
            w_uv = uv_ref[head]
            base = head * (nope + value)
            absorbed = dot(q_nope, w_uk).astype(bf16)
            d_out_latent = dot(grads, w_uv).astype(bf16)
            content = keys_ref[:, :rank]
            scores = dot_t(content, absorbed) + dot_t(keys_ref[:, rank:], q_rope)
            scores = scores * to_log2 + bias_ref[...]
            weights = jnp.exp2(scores - jnp.max(scores, axis=0, keepdims=True))
            probs = weights * (1.0 / jnp.sum(weights, axis=0, keepdims=True))
            low = probs.astype(bf16)
            out_t = dot(keys_t_ref[:rank, :], low).astype(bf16)
            att_t = dot(w_uv, out_t)
            att_ref[:, head * value : (head + 1) * value] = att_t.T.astype(bf16)
            own[step, base + nope : base + nope + value] = dot_t(grads.T, out_t).astype(bf16)
            d_probs = dot_t(content, d_out_latent)
            delta = jnp.sum(probs * d_probs, axis=0, keepdims=True)
            d_scores = (probs * (d_probs - delta) * inv_root).astype(bf16)
            d_full_t = dot(keys_t_ref[...], d_scores)
            d_absorbed_t = d_full_t[:rank].astype(bf16)
            d_nope_t = dot(w_uk, d_absorbed_t)
            dq_ref[:, head * width : (head + 1) * width] = jnp.concatenate(
                [d_nope_t, d_full_t[rank:]], axis=0
            ).T.astype(bf16)
            own[step, base : base + nope] = dot_t(q_nope.T, d_absorbed_t).astype(bf16)
            dkeys[:, :rank] += dot(d_scores, absorbed) + dot(low, d_out_latent)
            dkeys[:, rank:] += dot(d_scores, q_rope)
        pair_copy(step).start()

    @pl.when(step == steps - 1)
    def _():
        for back in range(SPAN + 1):
            sent[back] = dkeys[back * tok : (back + 1) * tok, :].astype(bf16)
        for d in range(1, peers):
            head_copy(d).start()

    at1 = step - LAGS[0]

    @pl.when((at1 >= 0) & (at1 < steps))
    def _():
        pair_copy(at1).wait()
        mine = own[at1, half_rows(parity)].astype(f32)
        mid[at1] = (mine + from_pair[at1].astype(f32)).astype(bf16)
        for d in range(1, line):
            line_copy(at1, d).start()

    at2 = step - LAGS[1]

    @pl.when((at2 >= 0) & (at2 < steps))
    def _():
        total = mid[at2, part_rows(place)].astype(f32)
        for d in range(1, line):
            line_copy(at2, d).wait()
            total = total + from_line[at2, d - 1].astype(f32)
        rows = pl.ds(pl.multiple_of(parity * half + place * part, 16), part)
        final[at2, rows] = total.astype(bf16)
        for d in range(1, line):
            back_copy(at2, d).start()

    at3 = step - LAGS[2]

    @pl.when((at3 >= 0) & (at3 < steps))
    def _():
        for d in range(1, line):
            back_copy(at3, d).wait()
        last_copy(at3).start()

    at4 = step - LAGS[3]

    @pl.when((at4 >= 0) & (at4 < steps))
    def _():
        last_copy(at4).wait()
        for head in range(PAIR):
            base = head * (nope + value)
            duk_ref[head] = final[at4, base : base + nope]
            duv_ref[head] = final[at4, base + nope : base + nope + value]

    own_rows = pl.ds(pl.multiple_of(head_me * quarter, 16), quarter)

    @pl.when(step == steps)
    def _():
        for d in range(1, peers):
            head_copy(d).wait()
        for back in range(1, SPAN + 1):
            block = sent[back, own_rows, :].astype(f32)
            for d in range(1, peers):
                block = block + from_head[d - 1, back].astype(f32)
            shifts[back - 1] = block.astype(bf16)

            @pl.when(me >= back)
            def _():
                ctx_copy(back).start()

        from_ctx_zero = jnp.zeros_like(from_ctx[0])
        for back in range(1, SPAN + 1):

            @pl.when(me + back >= n)
            def _():
                from_ctx[back - 1] = from_ctx_zero

    @pl.when(step == steps + 1)
    def _():
        block = sent[0, own_rows, :].astype(f32)
        for d in range(1, peers):
            block = block + from_head[d - 1, 0].astype(f32)
        for back in range(1, SPAN + 1):

            @pl.when(me >= back)
            def _():
                ctx_copy(back).wait_send()

            @pl.when(me + back < n)
            def _():
                ctx_copy(back).wait_recv()

            block = block + from_ctx[back - 1].astype(f32)
        gathered[own_rows] = block.astype(bf16)
        for d in range(1, peers):
            out_copy(d).start()

    @pl.when(step == steps + 3)
    def _():
        for d in range(1, peers):
            out_copy(d).wait()
        dlat_ref[...] = gathered[...]


def attend(n, peers, keys, keys_t, bias, query, d_out, w_uk, w_uv):
    tok = query.shape[0]
    heads, nope, rank = w_uk.shape
    value = w_uv.shape[1]
    width = query.shape[1] // heads
    span, lat = keys.shape
    steps = heads // PAIR
    rows = PAIR * (nope + value)
    half = rows // 2
    line = n // 2
    part = half // line
    quarter = tok // peers
    bf16 = jnp.bfloat16
    fixed = lambda i: (0, 0)
    columns = lambda i: (0, jnp.minimum(i, steps - 1))
    weight = lambda i: (jnp.minimum(i, steps - 1), 0, 0)
    late = lambda i: (jnp.maximum(i - LAGS[3], 0), 0, 0)
    flops = 2 * tok * heads * (span * (3 * lat + 3 * rank) + 6 * nope * rank)
    sem = pltpu.SemaphoreType.DMA
    return pl.pallas_call(
        functools.partial(
            attention_kernel, nope, width - nope, rank, value, steps, n, peers
        ),
        grid=(steps + LAGS[3],),
        in_specs=[
            pl.BlockSpec((span, lat), fixed),
            pl.BlockSpec((lat, span), fixed),
            pl.BlockSpec((span, tok), fixed),
            pl.BlockSpec((tok, PAIR * width), columns),
            pl.BlockSpec((tok, PAIR * value), columns),
            pl.BlockSpec((PAIR, nope, rank), weight),
            pl.BlockSpec((PAIR, value, rank), weight),
        ],
        out_specs=[
            pl.BlockSpec((tok, PAIR * value), columns),
            pl.BlockSpec((tok, PAIR * width), columns),
            pl.BlockSpec((tok, lat), fixed),
            pl.BlockSpec((PAIR, nope, rank), late),
            pl.BlockSpec((PAIR, value, rank), late),
        ],
        out_shape=[
            jax.ShapeDtypeStruct((tok, heads * value), bf16),
            jax.ShapeDtypeStruct((tok, heads * width), bf16),
            jax.ShapeDtypeStruct((tok, lat), bf16),
            jax.ShapeDtypeStruct((heads, nope, rank), bf16),
            jax.ShapeDtypeStruct((heads, value, rank), bf16),
        ],
        scratch_shapes=[
            pltpu.VMEM((span, lat), jnp.float32),
            pltpu.VMEM((steps, rows, rank), bf16),
            pltpu.VMEM((steps, half, rank), bf16),
            pltpu.VMEM((steps, half, rank), bf16),
            pltpu.VMEM((steps, line - 1, part, rank), bf16),
            pltpu.VMEM((steps, rows, rank), bf16),
            pltpu.VMEM((SPAN + 1, tok, lat), bf16),
            pltpu.VMEM((peers - 1, SPAN + 1, quarter, lat), bf16),
            pltpu.VMEM((SPAN, quarter, lat), bf16),
            pltpu.VMEM((SPAN, quarter, lat), bf16),
            pltpu.VMEM((tok, lat), bf16),
            sem((steps,)), sem((steps,)),
            sem((steps, line - 1)), sem((steps, line - 1)),
            sem((steps, line - 1)), sem((steps, line - 1)),
            sem((steps,)), sem((steps,)),
            sem((peers - 1,)), sem((peers - 1,)),
            sem((SPAN,)), sem((SPAN,)),
            sem((peers - 1,)), sem((peers - 1,)),
        ],
        compiler_params=pltpu.CompilerParams(
            vmem_limit_bytes=52 * 1024 * 1024, collective_id=0, has_side_effects=True
        ),
        cost_estimate=pl.CostEstimate(
            flops=flops, bytes_accessed=16 * span * lat, transcendentals=tok * heads * span
        ),
    )(keys, keys_t, bias, query, d_out, w_uk, w_uv)


def shifted(block, axis, distance):
    devices = range(lax.axis_size(axis))
    route = [(i - distance, i) for i in devices if i - distance in devices]
    return lax.ppermute(block, axis, route)


def mask_bias(tok, block_mask, segments):
    position = lax.axis_index("ctx")
    offsets = jnp.arange(tok, dtype=jnp.int32)
    seg_query = lax.dynamic_slice_in_dim(segments, position * tok, tok)
    parts = []
    for back in range(SPAN + 1):
        block = position - back
        clamped = jnp.maximum(block, 0)
        seg_key = lax.dynamic_slice_in_dim(segments, clamped * tok, tok)
        granted = block_mask[position, clamped] == 1
        allowed = (block >= 0) & ((seg_query[None, :] == seg_key[:, None]) | granted)
        if back == 0:
            allowed = allowed & (offsets[:, None] <= offsets[None, :])
        parts.append(jnp.where(allowed, 0.0, -jnp.inf).astype(jnp.float32))
    return jnp.concatenate(parts, axis=0)


def body(latent, query, d_out, w_uk, w_uv, block_mask, segments):
    tok = latent.shape[0]
    bias = mask_bias(tok, block_mask, segments)
    keys = jnp.concatenate([latent] + [shifted(latent, "ctx", d) for d in range(1, SPAN + 1)], axis=0)
    att, dq, d_latent, d_w_uk, d_w_uv = attend(
        lax.axis_size("ctx"), lax.axis_size("head"), keys, keys.T, bias, query, d_out, w_uk, w_uv
    )
    wide = jnp.float32
    return att, dq, d_latent.astype(wide), d_w_uk.astype(wide), d_w_uv.astype(wide)


def solution(mesh):
    in_specs = (
        P("ctx", None),
        P("ctx", "head"),
        P("ctx", "head"),
        P("head", None, None),
        P("head", None, None),
        P(),
        P(),
    )
    out_specs = (
        P("ctx", "head"),
        P("ctx", "head"),
        P("ctx", None),
        P("head", None, None),
        P("head", None, None),
    )
    return jax.shard_map(body, mesh=mesh, in_specs=in_specs, out_specs=out_specs, check_vma=False)
```

time: 421 us -> 154 us (0.37)
  waiting for transfers between devices: 302 us -> 4.58 us
  Pallas kernels: 60.2 us -> 122 us
  between operations: 16.9 us -> 2.68 us
  local copies, waits for them, and re-layouts: 14 us -> 7.77 us
  blocking collectives: 6.18 us -> 0 us
  starting transfers between devices: 12.1 us -> 6.95 us
    psum x4 -> x0, waiting for transfers between devices: 254 us -> none  [body(): uk, uv = lax.psum((uk, uv), 'ctx')]
    pallas_call x4 -> x1, Pallas kernels: 60.2 us -> 122 us  [attend(): pl.pallas_call(functools.partial(attention_kernel, nope, width - nope, ra...]
    unnamed x6 -> x0, waiting for transfers between devices: 39.4 us -> none
    all_gather x1 -> x0, blocking collectives: 6.18 us -> none  [body(): lax.all_gather(total.astype(jnp.bfloat16), 'head', axis=0, tiled=True)]
    ppermute x4 -> x2, waiting for transfers between devices: 9.44 us -> 4.58 us  [shifted(): return lax.ppermute(block, axis, route)]
    ppermute x4 -> x2, starting transfers between devices: 11.8 us -> 6.95 us  [shifted(): return lax.ppermute(block, axis, route)]
  transfers between devices with their start and end apart: 9 -> 2, of which waited for: 8 -> 1; matrix products, arithmetic and copies ran while one was open for 3% -> 2% of each run, Pallas kernels for 11% -> 0%
where the time goes in v2:
time: 154 us; the launch traced here: 152 us
  Pallas kernels  122 us (79%)
  local copies, waits for them, and re-layouts  7.77 us (5%)
  other arithmetic  7.19 us (5%)
  starting transfers between devices  6.95 us (5%)
  waiting for transfers between devices  4.58 us (3%)
  between operations  2.68 us (2%)
    pallas_call x1, Pallas kernels, attend(): pl.pallas_call(functools.partial(attention_kernel, nope, width - nope, ra...  122 us
    ppermute x2, starting transfers between devices, shifted(): return lax.ppermute(block, axis, route)  6.95 us
    ppermute x2, waiting for transfers between devices, shifted(): return lax.ppermute(block, axis, route)  4.58 us
    convert_element_type x1, other arithmetic, body(): d_w_uk.astype(wide)  4.32 us
    unnamed x11, local copies, waits for them, and re-layouts  4.11 us
  transfers between devices with their start and end apart: 2, of which 1 were waited for; matrix products, arithmetic and copies ran while one was open for 2% of the time, Pallas kernels for 0%

profile of v2, /device:TPU:14, one launch (start us, length us, event | category | flops | bytes accessed | tf_op | source)
XLA Modules:
  0.0 151.6 jit_solution(11898274310312079123)
XLA Ops:
  0.6 3.5 %collective-permute-start = (bf16[256,576]{0,1:T(8,128)(2,1)}, bf16[256,576]{0,1:T(8,128)(2,1)S(1)}, u32[]{:S(2)}, u32[]{:S(2)}) collective-permute-start(bf16[256,576]{0,1:T(8,128)(2,1)} %param.7), channel_id=1, source_target_pairs={{0,4},{4,8},{8,12},{12,16},{16,20},{20,24},{24,28},{1,5},{5,9},{9,... | collective-permute-start | bytes 884744 | tf_op jit(solution)/shard_map/ppermute | solution.py:338
  4.1 3.5 %collective-permute-start.1 = (bf16[256,576]{0,1:T(8,128)(2,1)}, bf16[256,576]{0,1:T(8,128)(2,1)S(1)}, u32[]{:S(2)}, u32[]{:S(2)}) collective-permute-start(bf16[256,576]{0,1:T(8,128)(2,1)} %param.7), channel_id=1, source_target_pairs={{0,8},{4,12},{8,16},{12,20},{16,24},{20,28},{1,9},{5,13},{9,17},{1... | collective-permute-start | bytes 884744 | tf_op jit(solution)/shard_map/ppermute | solution.py:338
  7.6 1.4 fusion.3
  11.0 0.9 fusion.2
  11.9 0.2 fusion.1
  12.1 1.0 constant_dynamic-update-slice_fusion.2
  13.1 0.1 pad_maximum_fusion.bias_ref
  13.2 0.0 collective-permute-done
  13.2 4.6 %collective-permute-done.1 = bf16[256,576]{0,1:T(8,128)(2,1)S(1)} collective-permute-done((bf16[256,576]{0,1:T(8,128)(2,1)}, bf16[256,576]{0,1:T(8,128)(2,1)S(1)}, u32[]{:S(2)}, u32[]{:S(2)}) %collective-permute-start.1) | collective-permute-done | bytes 294944 | tf_op jit(solution)/shard_map/ppermute | solution.py:338
  17.8 1.3 copy.12.keys_ref
  19.1 122.4 %shard_map.110 = (bf16[256,2048]{1,0:T(8,128)(2,1)}, bf16[256,3072]{1,0:T(8,128)(2,1)}, bf16[256,576]{1,0:T(8,128)(2,1)S(1)}, bf16[16,128,512]{2,1,0:T(8,128)(2,1)}, bf16[16,128,512]{2,1,0:T(8,128)(2,1)}) custom-call(bf16[768,576]{1,0:T(8,128)(2,1)} %copy.12.keys_ref, bf16[576,768]{1,0:T(8,128)(2,1)S(1)} %bitcast.4, ...), custom_call_target="tpu_custom_call" | custom-call | flops 23756537856 | bytes 7077888 | tf_op jit(solution)/shard_map/pallas_call | solution.py:278
  141.5 0.0 copy-start
  141.5 4.3 %convert_element_type.10 = f32[16,128,512]{2,1,0:T(8,128)} convert(bf16[16,128,512]{2,1,0:T(8,128)(2,1)} %get-tuple-element.13) | non-fusion elementwise | flops 1048576 | bytes 6291456 | tf_op jit(solution)/shard_map/convert_element_type | solution.py:366
  145.9 0.0 copy-done
  145.9 0.0 copy-start.2
  145.9 2.6 %convert_element_type.11 = f32[16,128,512]{2,1,0:T(8,128)} convert(bf16[16,128,512]{2,1,0:T(8,128)(2,1)S(1)} %copy-done) | non-fusion elementwise | flops 1048576 | bytes 6291456 | tf_op jit(solution)/shard_map/convert_element_type | solution.py:366
  148.5 0.0 copy-start.1
  148.5 1.0 copy.13
  149.4 0.0 copy-done.2
  149.4 1.0 copy.18
  150.4 0.0 copy-done.1
  150.4 1.1 copy.19
  (2 shorter events, 0.0 us)
Async XLA Ops:
  0.6 12.5 %collective-permute-start = (bf16[256,576]{0,1:T(8,128)(2,1)}, bf16[256,576]{0,1:T(8,128)(2,1)S(1)}, u32[]{:S(2)}, u32[]{:S(2)}) collective-permute-start(bf16[256,576]{0,1:T(8,128)(2,1)} %param.7), channel_id=1, source_target_pairs={{0,4},{4,8},{8,12},{12,16},{16,20},{20,24},{24,28},{1,5},{5,9},{9,... | collective-permute-start | bytes 884744 | tf_op jit(solution)/shard_map/ppermute | solution.py:338
  4.1 13.7 %collective-permute-start.1 = (bf16[256,576]{0,1:T(8,128)(2,1)}, bf16[256,576]{0,1:T(8,128)(2,1)S(1)}, u32[]{:S(2)}, u32[]{:S(2)}) collective-permute-start(bf16[256,576]{0,1:T(8,128)(2,1)} %param.7), channel_id=1, source_target_pairs={{0,8},{4,12},{8,16},{12,20},{16,24},{20,28},{1,9},{5,13},{9,17},{1... | collective-permute-start | bytes 884744 | tf_op jit(solution)/shard_map/ppermute | solution.py:338
  141.5 4.3 %copy-start = (bf16[16,128,512]{2,1,0:T(8,128)(2,1)S(1)}, bf16[16,128,512]{2,1,0:T(8,128)(2,1)}, u32[]{:S(2)}) copy-start(bf16[16,128,512]{2,1,0:T(8,128)(2,1)} %get-tuple-element.14) | copy-start | bytes 6291460
  145.9 3.6 %copy-start.2 = (bf16[256,2048]{1,0:T(8,128)(2,1)S(1)}, bf16[256,2048]{1,0:T(8,128)(2,1)}, u32[]{:S(2)}) copy-start(bf16[256,2048]{1,0:T(8,128)(2,1)} %get-tuple-element.35) | copy-start | bytes 3145732
  148.5 2.0 %copy-start.1 = (bf16[256,3072]{1,0:T(8,128)(2,1)S(1)}, bf16[256,3072]{1,0:T(8,128)(2,1)}, u32[]{:S(2)}) copy-start(bf16[256,3072]{1,0:T(8,128)(2,1)} %get-tuple-element.36) | copy-start | bytes 4718596

commit v3 on v2

--- a/solution.py
+++ b/solution.py
@@ -10,7 +10,7 @@
 
 SPAN = 2
 PAIR = 2
-LAGS = (1, 2, 4, 6)
+LAGS = (1, 3, 6, 8)
 
 
 def dot(a, b):
@@ -23,11 +23,11 @@
 
 def attention_kernel(
     nope, rope, rank, value, steps, n, peers,
-    keys_ref, keys_t_ref, bias_ref, query_ref, grads_ref, uk_ref, uv_ref,
+    lat_t_ref, bias_ref, query_ref, grads_ref, uk_ref, uv_ref,
     att_ref, dq_ref, dlat_ref, duk_ref, duv_ref,
-    dkeys, own, from_pair, mid, from_line, final, sent, from_head, shifts, from_ctx, gathered,
+    keys_ref, keys_t_ref, dkeys, own, from_pair, mid, from_line, final, sent, from_head, shifts, from_ctx, gathered,
     pair_send, pair_recv, line_send, line_recv, back_send, back_recv, last_send, last_recv,
-    head_send, head_recv, ctx_send, ctx_recv, out_send, out_recv,
+    head_send, head_recv, ctx_send, ctx_recv, out_send, out_recv, key_send, key_recv,
 ):
     bf16, f32 = jnp.bfloat16, jnp.float32
     width = nope + rope
@@ -106,9 +106,14 @@
             out_send.at[d - 1], out_recv.at[d - 1], {"head": peer},
         )
 
+    def key_copy(d):
+        return remote(
+            keys_t_ref.at[:, :tok], keys_t_ref.at[:, d * tok : (d + 1) * tok],
+            key_send.at[d - 1], key_recv.at[d - 1], {"ctx": lax.rem(me + d, n)},
+        )
+
     @pl.when(step == 0)
     def _():
-        dkeys[...] = jnp.zeros_like(dkeys)
         barrier = pltpu.get_barrier_semaphore()
         for d in range(1, n):
             pl.semaphore_signal(
@@ -120,7 +125,34 @@
                 barrier, inc=1, device_id={"head": lax.rem(head_me + d, peers)},
                 device_id_type=pl.DeviceIdType.MESH,
             )
+        keys_t_ref[:, :tok] = lat_t_ref[...]
         pl.semaphore_wait(barrier, n - 1 + peers - 1)
+        for d in range(1, SPAN + 1):
+
+            @pl.when(me + d < n)
+            def _():
+                key_copy(d).start()
+
+            @pl.when(me < d)
+            def _():
+                keys_t_ref[:, d * tok : (d + 1) * tok] = jnp.zeros(
+                    (keys_t_ref.shape[0], tok), keys_t_ref.dtype
+                )
+
+        dkeys[...] = jnp.zeros_like(dkeys)
+        keys_ref[:tok, :] = lat_t_ref[...].T
+        for d in range(1, SPAN + 1):
+
+            @pl.when(me >= d)
+            def _():
+                key_copy(d).wait_recv()
+
+            keys_ref[d * tok : (d + 1) * tok, :] = keys_t_ref[:, d * tok : (d + 1) * tok].T
+        for d in range(1, SPAN + 1):
+
+            @pl.when(me + d < n)
+            def _():
+                key_copy(d).wait_send()
 
     @pl.when(step < steps)
     def _():
@@ -256,12 +288,13 @@
         dlat_ref[...] = gathered[...]
 
 
-def attend(n, peers, keys, keys_t, bias, query, d_out, w_uk, w_uv):
+def attend(n, peers, lat_t, bias, query, d_out, w_uk, w_uv):
     tok = query.shape[0]
     heads, nope, rank = w_uk.shape
     value = w_uv.shape[1]
     width = query.shape[1] // heads
-    span, lat = keys.shape
+    lat = lat_t.shape[0]
+    span = bias.shape[0]
     steps = heads // PAIR
     rows = PAIR * (nope + value)
     half = rows // 2
@@ -281,8 +314,7 @@
         ),
         grid=(steps + LAGS[3],),
         in_specs=[
-            pl.BlockSpec((span, lat), fixed),
-            pl.BlockSpec((lat, span), fixed),
+            pl.BlockSpec((lat, tok), fixed),
             pl.BlockSpec((span, tok), fixed),
             pl.BlockSpec((tok, PAIR * width), columns),
             pl.BlockSpec((tok, PAIR * value), columns),
@@ -304,6 +336,8 @@
             jax.ShapeDtypeStruct((heads, value, rank), bf16),
         ],
         scratch_shapes=[
+            pltpu.VMEM((span, lat), bf16),
+            pltpu.VMEM((lat, span), bf16),
             pltpu.VMEM((span, lat), jnp.float32),
             pltpu.VMEM((steps, rows, rank), bf16),
             pltpu.VMEM((steps, half, rank), bf16),
@@ -322,6 +356,7 @@
             sem((peers - 1,)), sem((peers - 1,)),
             sem((SPAN,)), sem((SPAN,)),
             sem((peers - 1,)), sem((peers - 1,)),
+            sem((SPAN,)), sem((SPAN,)),
         ],
         compiler_params=pltpu.CompilerParams(
             vmem_limit_bytes=52 * 1024 * 1024, collective_id=0, has_side_effects=True
@@ -329,13 +364,7 @@
         cost_estimate=pl.CostEstimate(
             flops=flops, bytes_accessed=16 * span * lat, transcendentals=tok * heads * span
         ),
-    )(keys, keys_t, bias, query, d_out, w_uk, w_uv)
-
-
-def shifted(block, axis, distance):
-    devices = range(lax.axis_size(axis))
-    route = [(i - distance, i) for i in devices if i - distance in devices]
-    return lax.ppermute(block, axis, route)
+    )(lat_t, bias, query, d_out, w_uk, w_uv)
 
 
 def mask_bias(tok, block_mask, segments):
@@ -358,9 +387,8 @@
 def body(latent, query, d_out, w_uk, w_uv, block_mask, segments):
     tok = latent.shape[0]
     bias = mask_bias(tok, block_mask, segments)
-    keys = jnp.concatenate([latent] + [shifted(latent, "ctx", d) for d in range(1, SPAN + 1)], axis=0)
     att, dq, d_latent, d_w_uk, d_w_uv = attend(
-        lax.axis_size("ctx"), lax.axis_size("head"), keys, keys.T, bias, query, d_out, w_uk, w_uv
+        lax.axis_size("ctx"), lax.axis_size("head"), latent.T, bias, query, d_out, w_uk, w_uv
     )
     wide = jnp.float32
     return att, dq, d_latent.astype(wide), d_w_uk.astype(wide), d_w_uv.astype(wide)

time: 154 us -> 160 us (1.039); the launches traced: 152 us -> 160 us
  Pallas kernels: 122 us -> 145 us
  starting transfers between devices: 6.95 us -> 0 us
  waiting for transfers between devices: 4.58 us -> 0 us
  local copies, waits for them, and re-layouts: 7.77 us -> 5.41 us
    pallas_call x1, Pallas kernels: 122 us -> 145 us  [attend(): pl.pallas_call(functools.partial(attention_kernel, nope, width - nope, ra...]
    ppermute x2 -> x0, starting transfers between devices: 6.95 us -> none  [shifted(): return lax.ppermute(block, axis, route)]
    ppermute x2 -> x0, waiting for transfers between devices: 4.58 us -> none  [shifted(): return lax.ppermute(block, axis, route)]
  transfers between devices with their start and end apart: 2 -> 0, of which waited for: 1 -> 0; matrix products, arithmetic and copies ran while one was open for 2% -> 0% of each run, Pallas kernels for 0% -> 0%
where the time goes in v3:
time: 160 us
  Pallas kernels  145 us (91%)
  other arithmetic  7.19 us (4%)
  local copies, waits for them, and re-layouts  5.41 us (3%)
  between operations  2.66 us (2%)
    pallas_call x1, Pallas kernels, attend(): pl.pallas_call(functools.partial(attention_kernel, nope, width - nope, ra...  145 us
    convert_element_type x1, other arithmetic, body(): d_w_uk.astype(wide)  4.32 us

profile of v3, /device:TPU:14, one launch (start us, length us, event | category | flops | bytes accessed | tf_op | source)
XLA Modules:
  0.0 160.1 jit_solution(16793448116525868025)
XLA Ops:
  0.6 0.0 copy-start
  0.7 0.9 fusion.2
  1.6 1.4 fusion.3
  4.9 0.2 fusion.1
  5.2 0.1 pad_maximum_fusion.bias_ref
  5.2 0.0 copy-done
  5.2 144.8 %shard_map.110 = (bf16[256,2048]{1,0:T(8,128)(2,1)}, bf16[256,3072]{1,0:T(8,128)(2,1)}, bf16[256,576]{1,0:T(8,128)(2,1)S(1)}, bf16[16,128,512]{2,1,0:T(8,128)(2,1)}, bf16[16,128,512]{2,1,0:T(8,128)(2,1)}) custom-call(bf16[576,256]{1,0:T(8,128)(2,1)S(1)} %bitcast.4, f32[768,256]{1,0:T(8,128)S(1)} %pad_maximum_fusion.bias_ref, bf16[256,3072]{1,0:T(8,128)(2,1)} %query_ref.1, ...), custom_call_target="tpu_custom_call" | custom-call | flops 23756537856 | bytes 7077888 | tf_op jit(solution)/shard_map/pallas_call | solution.py:311
  150.0 0.0 copy-start.1
  150.0 4.3 %convert_element_type.10 = f32[16,128,512]{2,1,0:T(8,128)} convert(bf16[16,128,512]{2,1,0:T(8,128)(2,1)} %get-tuple-element.13) | non-fusion elementwise | flops 1048576 | bytes 6291456 | tf_op jit(solution)/shard_map/convert_element_type | solution.py:394
  154.4 0.0 copy-done.1
  154.4 0.0 copy-start.3
  154.4 2.6 %convert_element_type.11 = f32[16,128,512]{2,1,0:T(8,128)} convert(bf16[16,128,512]{2,1,0:T(8,128)(2,1)S(1)} %copy-done.1) | non-fusion elementwise | flops 1048576 | bytes 6291456 | tf_op jit(solution)/shard_map/convert_element_type | solution.py:394
  157.0 0.0 copy-start.2
  157.0 1.0 copy.12
  157.9 0.0 copy-done.3
  157.9 1.0 copy.15
  158.9 0.0 copy-done.2
  158.9 1.1 copy.16
Async XLA Ops:
  0.6 4.6 %copy-start = (bf16[256,576]{0,1:T(8,128)(2,1)S(1)}, bf16[256,576]{0,1:T(8,128)(2,1)}, u32[]{:S(2)}) copy-start(bf16[256,576]{0,1:T(8,128)(2,1)} %param.7) | copy-start | bytes 884740
  150.0 4.3 %copy-start.1 = (bf16[16,128,512]{2,1,0:T(8,128)(2,1)S(1)}, bf16[16,128,512]{2,1,0:T(8,128)(2,1)}, u32[]{:S(2)}) copy-start(bf16[16,128,512]{2,1,0:T(8,128)(2,1)} %get-tuple-element.14) | copy-start | bytes 6291460
  154.4 3.6 %copy-start.3 = (bf16[256,2048]{1,0:T(8,128)(2,1)S(1)}, bf16[256,2048]{1,0:T(8,128)(2,1)}, u32[]{:S(2)}) copy-start(bf16[256,2048]{1,0:T(8,128)(2,1)} %get-tuple-element.35) | copy-start | bytes 3145732
  157.0 2.0 %copy-start.2 = (bf16[256,3072]{1,0:T(8,128)(2,1)S(1)}, bf16[256,3072]{1,0:T(8,128)(2,1)}, u32[]{:S(2)}) copy-start(bf16[256,3072]{1,0:T(8,128)(2,1)} %get-tuple-element.36) | copy-start | bytes 4718596

commit v4 on v3

--- a/solution.py
+++ b/solution.py
@@ -10,7 +10,7 @@
 
 SPAN = 2
 PAIR = 2
-LAGS = (1, 3, 6, 8)
+LAGS = (1, 2, 4, 6)
 
 
 def dot(a, b):
@@ -28,6 +28,7 @@
     keys_ref, keys_t_ref, dkeys, own, from_pair, mid, from_line, final, sent, from_head, shifts, from_ctx, gathered,
     pair_send, pair_recv, line_send, line_recv, back_send, back_recv, last_send, last_recv,
     head_send, head_recv, ctx_send, ctx_recv, out_send, out_recv, key_send, key_recv,
+    share_send, share_recv,
 ):
     bf16, f32 = jnp.bfloat16, jnp.float32
     width = nope + rope
@@ -106,10 +107,21 @@
             out_send.at[d - 1], out_recv.at[d - 1], {"head": peer},
         )
 
+    core = lax.rem(head_me, 2)
+    core_half = keys_t_ref.shape[0] // 2
+    core_rows = pl.ds(pl.multiple_of(core * core_half, 16), core_half)
+
     def key_copy(d):
         return remote(
-            keys_t_ref.at[:, :tok], keys_t_ref.at[:, d * tok : (d + 1) * tok],
+            keys_t_ref.at[core_rows, :tok], keys_t_ref.at[core_rows, d * tok : (d + 1) * tok],
             key_send.at[d - 1], key_recv.at[d - 1], {"ctx": lax.rem(me + d, n)},
+        )
+
+    def share_copy(d):
+        block = keys_t_ref.at[core_rows, d * tok : (d + 1) * tok]
+        return remote(
+            block, block, share_send.at[d - 1], share_recv.at[d - 1],
+            {"head": head_me + 1 - 2 * core},
         )
 
     @pl.when(step == 0)
@@ -146,6 +158,13 @@
             @pl.when(me >= d)
             def _():
                 key_copy(d).wait_recv()
+                share_copy(d).start()
+
+        for d in range(1, SPAN + 1):
+
+            @pl.when(me >= d)
+            def _():
+                share_copy(d).wait()
 
             keys_ref[d * tok : (d + 1) * tok, :] = keys_t_ref[:, d * tok : (d + 1) * tok].T
         for d in range(1, SPAN + 1):
@@ -357,6 +376,7 @@
             sem((SPAN,)), sem((SPAN,)),
             sem((peers - 1,)), sem((peers - 1,)),
             sem((SPAN,)), sem((SPAN,)),
+            sem((SPAN,)), sem((SPAN,)),
         ],
         compiler_params=pltpu.CompilerParams(
             vmem_limit_bytes=52 * 1024 * 1024, collective_id=0, has_side_effects=True

time: 160 us -> 151 us (0.944)
  Pallas kernels: 145 us -> 136 us
    pallas_call x1, Pallas kernels: 145 us -> 136 us  [attend(): pl.pallas_call(functools.partial(attention_kernel, nope, width - nope, ra...]
where the time goes in v4:
time: 151 us
  Pallas kernels  136 us (90%)
  other arithmetic  7.19 us (5%)
  local copies, waits for them, and re-layouts  5.41 us (4%)
  between operations  2.66 us (2%)
    pallas_call x1, Pallas kernels, attend(): pl.pallas_call(functools.partial(attention_kernel, nope, width - nope, ra...  136 us
    convert_element_type x1, other arithmetic, body(): d_w_uk.astype(wide)  4.32 us
    unnamed x11, local copies, waits for them, and re-layouts  3.1 us

profile of v4, /device:TPU:14, one launch (start us, length us, event | category | flops | bytes accessed | tf_op | source)
XLA Modules:
  0.0 150.9 jit_solution(12369023954426385038)
XLA Ops:
  0.6 0.0 copy-start
  0.7 0.9 fusion.2
  1.6 1.4 fusion.3
  4.9 0.2 fusion.1
  5.2 0.1 pad_maximum_fusion.bias_ref
  5.2 0.0 copy-done
  5.2 135.6 %shard_map.110 = (bf16[256,2048]{1,0:T(8,128)(2,1)}, bf16[256,3072]{1,0:T(8,128)(2,1)}, bf16[256,576]{1,0:T(8,128)(2,1)S(1)}, bf16[16,128,512]{2,1,0:T(8,128)(2,1)}, bf16[16,128,512]{2,1,0:T(8,128)(2,1)}) custom-call(bf16[576,256]{1,0:T(8,128)(2,1)S(1)} %bitcast.4, f32[768,256]{1,0:T(8,128)S(1)} %pad_maximum_fusion.bias_ref, bf16[256,3072]{1,0:T(8,128)(2,1)} %query_ref.1, ...), custom_call_target="tpu_custom_call" | custom-call | flops 23756537856 | bytes 7077888 | tf_op jit(solution)/shard_map/pallas_call | solution.py:330
  140.8 0.0 copy-start.1
  140.8 4.3 %convert_element_type.10 = f32[16,128,512]{2,1,0:T(8,128)} convert(bf16[16,128,512]{2,1,0:T(8,128)(2,1)} %get-tuple-element.13) | non-fusion elementwise | flops 1048576 | bytes 6291456 | tf_op jit(solution)/shard_map/convert_element_type | solution.py:414
  145.2 0.0 copy-done.1
  145.2 0.0 copy-start.3
  145.2 2.6 %convert_element_type.11 = f32[16,128,512]{2,1,0:T(8,128)} convert(bf16[16,128,512]{2,1,0:T(8,128)(2,1)S(1)} %copy-done.1) | non-fusion elementwise | flops 1048576 | bytes 6291456 | tf_op jit(solution)/shard_map/convert_element_type | solution.py:414
  147.8 0.0 copy-start.2
  147.8 1.0 copy.12
  148.7 0.0 copy-done.3
  148.7 1.0 copy.15
  149.7 0.0 copy-done.2
  149.7 1.1 copy.16
Async XLA Ops:
  0.6 4.6 %copy-start = (bf16[256,576]{0,1:T(8,128)(2,1)S(1)}, bf16[256,576]{0,1:T(8,128)(2,1)}, u32[]{:S(2)}) copy-start(bf16[256,576]{0,1:T(8,128)(2,1)} %param.7) | copy-start | bytes 884740
  140.8 4.3 %copy-start.1 = (bf16[16,128,512]{2,1,0:T(8,128)(2,1)S(1)}, bf16[16,128,512]{2,1,0:T(8,128)(2,1)}, u32[]{:S(2)}) copy-start(bf16[16,128,512]{2,1,0:T(8,128)(2,1)} %get-tuple-element.14) | copy-start | bytes 6291460
  145.2 3.6 %copy-start.3 = (bf16[256,2048]{1,0:T(8,128)(2,1)S(1)}, bf16[256,2048]{1,0:T(8,128)(2,1)}, u32[]{:S(2)}) copy-start(bf16[256,2048]{1,0:T(8,128)(2,1)} %get-tuple-element.35) | copy-start | bytes 3145732
  147.8 2.0 %copy-start.2 = (bf16[256,3072]{1,0:T(8,128)(2,1)S(1)}, bf16[256,3072]{1,0:T(8,128)(2,1)}, u32[]{:S(2)}) copy-start(bf16[256,3072]{1,0:T(8,128)(2,1)} %get-tuple-element.36) | copy-start | bytes 4718596

commit v5 on v4

--- a/solution.py
+++ b/solution.py
@@ -10,7 +10,6 @@
 
 SPAN = 2
 PAIR = 2
-LAGS = (1, 2, 4, 6)
 
 
 def dot(a, b):
@@ -22,11 +21,11 @@
 
 
 def attention_kernel(
-    nope, rope, rank, value, steps, n, peers,
+    nope, rope, rank, value, steps, n, peers, bits,
     lat_t_ref, bias_ref, query_ref, grads_ref, uk_ref, uv_ref,
     att_ref, dq_ref, dlat_ref, duk_ref, duv_ref,
-    keys_ref, keys_t_ref, dkeys, own, from_pair, mid, from_line, final, sent, from_head, shifts, from_ctx, gathered,
-    pair_send, pair_recv, line_send, line_recv, back_send, back_recv, last_send, last_recv,
+    keys_ref, keys_t_ref, dkeys, own, landing, final, sent, from_head, shifts, from_ctx, gathered,
+    sum_send, sum_recv,
     head_send, head_recv, ctx_send, ctx_recv, out_send, out_recv, key_send, key_recv,
     share_send, share_recv,
 ):
@@ -37,11 +36,7 @@
     step = pl.program_id(0)
     me = lax.axis_index("ctx")
     head_me = lax.axis_index("head")
-    parity = lax.rem(me, 2)
-    place = me // 2
-    line = n // 2
-    half = own.shape[1] // 2
-    part = half // line
+    rows = own.shape[1]
     tok = att_ref.shape[0]
     quarter = tok // peers
 
@@ -51,38 +46,38 @@
             device_id=target, device_id_type=pl.DeviceIdType.MESH,
         )
 
-    def half_rows(which):
-        return pl.ds(pl.multiple_of(which * half, 16), half)
-
-    def part_rows(at):
-        return pl.ds(pl.multiple_of(at * part, 16), part)
-
-    def pair_copy(c):
-        return remote(
-            own.at[c, half_rows(1 - parity)], from_pair.at[c],
-            pair_send.at[c], pair_recv.at[c], {"ctx": me + 1 - 2 * parity},
-        )
-
-    def line_copy(c, d):
-        peer = lax.rem(place + d, line)
-        return remote(
-            mid.at[c, part_rows(peer)], from_line.at[c, d - 1],
-            line_send.at[c, d - 1], line_recv.at[c, d - 1], {"ctx": peer * 2 + parity},
-        )
-
-    def back_copy(c, d):
-        peer = lax.rem(place + d, line)
-        rows = pl.ds(pl.multiple_of(parity * half + place * part, 16), part)
-        return remote(
-            final.at[c, rows], final.at[c, rows],
-            back_send.at[c, d - 1], back_recv.at[c, d - 1], {"ctx": peer * 2 + parity},
-        )
-
-    def last_copy(c):
-        rows = half_rows(parity)
-        return remote(
-            final.at[c, rows], final.at[c, rows],
-            last_send.at[c], last_recv.at[c], {"ctx": me + 1 - 2 * parity},
+    def stage(c, k):
+        turned = (lax.rem(c + 4, 8) + 1) // 8
+        stride = 2**k + turned * (2 ** ((k + 1) % bits) - 2**k)
+        return stride, lax.rem(me // stride, 2)
+
+    def partner(c, k):
+        stride, bit = stage(c, k)
+        return {"ctx": me + (1 - 2 * bit) * stride}
+
+    def offset(c, k):
+        at = 0
+        for j in range(k):
+            at = at + stage(c, j)[1] * (rows >> (j + 1))
+        return at
+
+    def region(at, k):
+        return pl.ds(pl.multiple_of(at, 16), rows >> k)
+
+    def landed(k):
+        return pl.ds(rows - (rows >> k), rows >> (k + 1))
+
+    def sum_copy(c, k):
+        other = offset(c, k) + (1 - stage(c, k)[1]) * (rows >> (k + 1))
+        return remote(
+            own.at[c, region(other, k + 1)], landing.at[c, landed(k)],
+            sum_send.at[c, k], sum_recv.at[c, k], partner(c, k),
+        )
+
+    def back_copy(c, k):
+        part = final.at[c, region(offset(c, k + 1), k + 1)]
+        return remote(
+            part, part, sum_send.at[c, bits + k], sum_recv.at[c, bits + k], partner(c, k)
         )
 
     def head_copy(d):
@@ -207,7 +202,7 @@
             own[step, base : base + nope] = dot_t(q_nope.T, d_absorbed_t).astype(bf16)
             dkeys[:, :rank] += dot(d_scores, absorbed) + dot(low, d_out_latent)
             dkeys[:, rank:] += dot(d_scores, q_rope)
-        pair_copy(step).start()
+        sum_copy(step, 0).start()
 
     @pl.when(step == steps - 1)
     def _():
@@ -216,46 +211,34 @@
         for d in range(1, peers):
             head_copy(d).start()
 
-    at1 = step - LAGS[0]
-
-    @pl.when((at1 >= 0) & (at1 < steps))
-    def _():
-        pair_copy(at1).wait()
-        mine = own[at1, half_rows(parity)].astype(f32)
-        mid[at1] = (mine + from_pair[at1].astype(f32)).astype(bf16)
-        for d in range(1, line):
-            line_copy(at1, d).start()
-
-    at2 = step - LAGS[1]
-
-    @pl.when((at2 >= 0) & (at2 < steps))
-    def _():
-        total = mid[at2, part_rows(place)].astype(f32)
-        for d in range(1, line):
-            line_copy(at2, d).wait()
-            total = total + from_line[at2, d - 1].astype(f32)
-        rows = pl.ds(pl.multiple_of(parity * half + place * part, 16), part)
-        final[at2, rows] = total.astype(bf16)
-        for d in range(1, line):
-            back_copy(at2, d).start()
-
-    at3 = step - LAGS[2]
-
-    @pl.when((at3 >= 0) & (at3 < steps))
-    def _():
-        for d in range(1, line):
-            back_copy(at3, d).wait()
-        last_copy(at3).start()
-
-    at4 = step - LAGS[3]
-
-    @pl.when((at4 >= 0) & (at4 < steps))
-    def _():
-        last_copy(at4).wait()
-        for head in range(PAIR):
-            base = head * (nope + value)
-            duk_ref[head] = final[at4, base : base + nope]
-            duv_ref[head] = final[at4, base + nope : base + nope + value]
+    for k in range(bits):
+        at = step - 1 - k
+
+        @pl.when((at >= 0) & (at < steps))
+        def _():
+            sum_copy(at, k).wait()
+            mine = region(offset(at, k + 1), k + 1)
+            total = own[at, mine].astype(f32) + landing[at, landed(k)].astype(f32)
+            if k + 1 < bits:
+                own[at, mine] = total.astype(bf16)
+                sum_copy(at, k + 1).start()
+            else:
+                final[at, mine] = total.astype(bf16)
+                back_copy(at, k).start()
+
+    for k in range(bits - 1, -1, -1):
+        at = step - 2 * bits + k
+
+        @pl.when((at >= 0) & (at < steps))
+        def _():
+            back_copy(at, k).wait()
+            if k > 0:
+                back_copy(at, k - 1).start()
+            else:
+                for head in range(PAIR):
+                    base = head * (nope + value)
+                    duk_ref[head] = final[at, base : base + nope]
+                    duv_ref[head] = final[at, base + nope : base + nope + value]
 
     own_rows = pl.ds(pl.multiple_of(head_me * quarter, 16), quarter)
 
@@ -316,22 +299,21 @@
     span = bias.shape[0]
     steps = heads // PAIR
     rows = PAIR * (nope + value)
-    half = rows // 2
-    line = n // 2
-    part = half // line
+    bits = n.bit_length() - 1
+    lag = 2 * bits
     quarter = tok // peers
     bf16 = jnp.bfloat16
     fixed = lambda i: (0, 0)
     columns = lambda i: (0, jnp.minimum(i, steps - 1))
     weight = lambda i: (jnp.minimum(i, steps - 1), 0, 0)
-    late = lambda i: (jnp.maximum(i - LAGS[3], 0), 0, 0)
+    late = lambda i: (jnp.maximum(i - lag, 0), 0, 0)
     flops = 2 * tok * heads * (span * (3 * lat + 3 * rank) + 6 * nope * rank)
     sem = pltpu.SemaphoreType.DMA
     return pl.pallas_call(
         functools.partial(
-            attention_kernel, nope, width - nope, rank, value, steps, n, peers
+            attention_kernel, nope, width - nope, rank, value, steps, n, peers, bits
         ),
-        grid=(steps + LAGS[3],),
+        grid=(steps + lag,),
         in_specs=[
             pl.BlockSpec((lat, tok), fixed),
             pl.BlockSpec((span, tok), fixed),
@@ -359,19 +341,14 @@
             pltpu.VMEM((lat, span), bf16),
             pltpu.VMEM((span, lat), jnp.float32),
             pltpu.VMEM((steps, rows, rank), bf16),
-            pltpu.VMEM((steps, half, rank), bf16),
-            pltpu.VMEM((steps, half, rank), bf16),
-            pltpu.VMEM((steps, line - 1, part, rank), bf16),
+            pltpu.VMEM((steps, rows, rank), bf16),
             pltpu.VMEM((steps, rows, rank), bf16),
             pltpu.VMEM((SPAN + 1, tok, lat), bf16),
             pltpu.VMEM((peers - 1, SPAN + 1, quarter, lat), bf16),
             pltpu.VMEM((SPAN, quarter, lat), bf16),
             pltpu.VMEM((SPAN, quarter, lat), bf16),
             pltpu.VMEM((tok, lat), bf16),
-            sem((steps,)), sem((steps,)),
-            sem((steps, line - 1)), sem((steps, line - 1)),
-            sem((steps, line - 1)), sem((steps, line - 1)),
-            sem((steps,)), sem((steps,)),
+            sem((steps, lag)), sem((steps, lag)),
             sem((peers - 1,)), sem((peers - 1,)),
             sem((SPAN,)), sem((SPAN,)),
             sem((peers - 1,)), sem((peers - 1,)),

time: 151 us -> 150 us (level); the launches traced: 151 us -> 147 us
  Pallas kernels: 136 us -> 132 us
    pallas_call x1, Pallas kernels: 136 us -> 132 us  [attend(): pl.pallas_call(functools.partial(attention_kernel, nope, width - nope, ra...]
where the time goes in v5:
time: 150 us; the launch traced here: 147 us
  Pallas kernels  132 us (88%)
  other arithmetic  7.19 us (5%)
  local copies, waits for them, and re-layouts  5.41 us (4%)
  between operations  2.66 us (2%)
    pallas_call x1, Pallas kernels, attend(): pl.pallas_call(functools.partial(attention_kernel, nope, width - nope, ra...  132 us
    convert_element_type x1, other arithmetic, body(): d_w_uk.astype(wide)  4.32 us
    unnamed x11, local copies, waits for them, and re-layouts  3.1 us

profile of v5, /device:TPU:14, one launch (start us, length us, event | category | flops | bytes accessed | tf_op | source)
XLA Modules:
  0.0 147.3 jit_solution(7348944981298498448)
XLA Ops:
  0.6 0.0 copy-start
  0.7 0.9 fusion.2
  1.6 1.4 fusion.3
  4.9 0.2 fusion.1
  5.2 0.1 pad_maximum_fusion.bias_ref
  5.2 0.0 copy-done
  5.2 132.0 %shard_map.110 = (bf16[256,2048]{1,0:T(8,128)(2,1)}, bf16[256,3072]{1,0:T(8,128)(2,1)}, bf16[256,576]{1,0:T(8,128)(2,1)S(1)}, bf16[16,128,512]{2,1,0:T(8,128)(2,1)}, bf16[16,128,512]{2,1,0:T(8,128)(2,1)}) custom-call(bf16[576,256]{1,0:T(8,128)(2,1)S(1)} %bitcast.4, f32[768,256]{1,0:T(8,128)S(1)} %pad_maximum_fusion.bias_ref, bf16[256,3072]{1,0:T(8,128)(2,1)} %query_ref.1, ...), custom_call_target="tpu_custom_call" | custom-call | flops 23756537856 | bytes 7077888 | tf_op jit(solution)/shard_map/pallas_call | solution.py:312
  137.3 0.0 copy-start.1
  137.3 4.3 %convert_element_type.10 = f32[16,128,512]{2,1,0:T(8,128)} convert(bf16[16,128,512]{2,1,0:T(8,128)(2,1)} %get-tuple-element.13) | non-fusion elementwise | flops 1048576 | bytes 6291456 | tf_op jit(solution)/shard_map/convert_element_type | solution.py:391
  141.6 0.0 copy-done.1
  141.6 0.0 copy-start.3
  141.6 2.6 %convert_element_type.11 = f32[16,128,512]{2,1,0:T(8,128)} convert(bf16[16,128,512]{2,1,0:T(8,128)(2,1)S(1)} %copy-done.1) | non-fusion elementwise | flops 1048576 | bytes 6291456 | tf_op jit(solution)/shard_map/convert_element_type | solution.py:391
  144.2 0.0 copy-start.2
  144.2 1.0 copy.12
  145.2 0.0 copy-done.3
  145.2 1.0 copy.15
  146.1 0.0 copy-done.2
  146.1 1.1 copy.16
Async XLA Ops:
  0.6 4.6 %copy-start = (bf16[256,576]{0,1:T(8,128)(2,1)S(1)}, bf16[256,576]{0,1:T(8,128)(2,1)}, u32[]{:S(2)}) copy-start(bf16[256,576]{0,1:T(8,128)(2,1)} %param.7) | copy-start | bytes 884740
  137.3 4.3 %copy-start.1 = (bf16[16,128,512]{2,1,0:T(8,128)(2,1)S(1)}, bf16[16,128,512]{2,1,0:T(8,128)(2,1)}, u32[]{:S(2)}) copy-start(bf16[16,128,512]{2,1,0:T(8,128)(2,1)} %get-tuple-element.14) | copy-start | bytes 6291460
  141.6 3.6 %copy-start.3 = (bf16[256,2048]{1,0:T(8,128)(2,1)S(1)}, bf16[256,2048]{1,0:T(8,128)(2,1)}, u32[]{:S(2)}) copy-start(bf16[256,2048]{1,0:T(8,128)(2,1)} %get-tuple-element.35) | copy-start | bytes 3145732
  144.2 2.0 %copy-start.2 = (bf16[256,3072]{1,0:T(8,128)(2,1)S(1)}, bf16[256,3072]{1,0:T(8,128)(2,1)}, u32[]{:S(2)}) copy-start(bf16[256,3072]{1,0:T(8,128)(2,1)} %get-tuple-element.36) | copy-start | bytes 4718596
